TPU v7x, 256 devices: a whole 4x4x8 slice. The times are simulated.
256 devices in a mesh: brick: 32 (over x, z), region: 8 (over y, core).
Axes of the slice: x: 4, y: 4, z: 8, core: 2. Of those that a mesh axis runs over, the one named last changes fastest.
Arguments:
- segments: float32 [8192, 8, 128], P(('brick', 'region'))
- ship_list: int32 [256, 32, 4], P(('brick', 'region')), may hold values from 0 to 31
- kept_tiles: int32 [256, 64, 2], P(('brick', 'region')), may hold values from 0 to 159
- kept_count: int32 [256], P(('brick', 'region')), may hold values from 1 to 64, as said below
- lent_tiles: int32 [256, 8, 8, 2], P(('brick', 'region')), may hold values from 0 to 159
- lent_count: int32 [32, 8, 8], P('brick'), may hold values from 0 to 8, as said below
Outputs:
- loads: float32 [8192, 6, 128], P(('brick', 'region'))
Inputs may be any that keep to these rules, and one draw needn't show every extreme that they name: `kept_count`: in every brick one device has exactly 64 live kept slots. `lent_count`: zero where i equals j; in every brick some entry equals 8.
All inputs are finite; a program needn't handle non-finite values.
Results may differ from a plain program's by a relative error of at most 0.0001.
Values sent between devices are 32-bit elements; how exact they have to be, the bound alone decides.
A program may use at most 64 MiB of HBM per device.

v0:
```python
import jax
import jax.numpy as jnp
from jax import lax
from jax.sharding import PartitionSpec as P

GROUP = 8
DIST_FLOOR = 0.0025
PARALLEL_FLOOR = 0.05


def cross_rows(lever, force):
    return jnp.stack(
        [
            lever[:, 1] * force[:, 2] - lever[:, 2] * force[:, 1],
            lever[:, 2] * force[:, 0] - lever[:, 0] * force[:, 2],
            lever[:, 0] * force[:, 1] - lever[:, 1] * force[:, 0],
        ],
        axis=1,
    )


def pair_forces(left, right):
    start_a = left[:, 0:3, :, None]
    axis_a = left[:, 3:6, :, None]
    radius_a = left[:, 6, :, None]
    modulus_a = left[:, 7, :, None]
    start_b = right[:, 0:3, None, :]
    axis_b = right[:, 3:6, None, :]
    radius_b = right[:, 6, None, :]
    modulus_b = right[:, 7, None, :]
    offset = start_a - start_b
    len_a = jnp.sum(axis_a * axis_a, axis=1)
    len_b = jnp.sum(axis_b * axis_b, axis=1)
    cosine = jnp.sum(axis_a * axis_b, axis=1)
    proj_a = jnp.sum(axis_a * offset, axis=1)
    proj_b = jnp.sum(axis_b * offset, axis=1)
    denom = jnp.maximum(len_a * len_b - cosine * cosine, PARALLEL_FLOOR * len_a * len_b)
    param_a = jnp.clip((cosine * proj_b - proj_a * len_b) / denom, 0.0, 1.0)
    param_b = jnp.clip((cosine * param_a + proj_b) / len_b, 0.0, 1.0)
    param_a = jnp.clip((cosine * param_b - proj_a) / len_a, 0.0, 1.0)
    gap = offset + param_a[:, None] * axis_a - param_b[:, None] * axis_b
    dist = jnp.sqrt(jnp.maximum(jnp.sum(gap * gap, axis=1), DIST_FLOOR))
    depth = jnp.maximum(radius_a + radius_b - dist, 0.0)
    stiff = (
        4.0
        / 3.0
        * modulus_a
        * modulus_b
        / (modulus_a + modulus_b)
        * jnp.sqrt(radius_a * radius_b / (radius_a + radius_b))
    )
    scale = stiff * depth * jnp.sqrt(depth) / dist
    force = scale[:, None] * gap
    torque_a = cross_rows((param_a - 0.5)[:, None] * axis_a, force)
    torque_b = cross_rows((param_b - 0.5)[:, None] * axis_b, -force)
    on_a = jnp.concatenate([jnp.sum(force, axis=3), jnp.sum(torque_a, axis=3)], axis=1)
    on_b = jnp.concatenate([-jnp.sum(force, axis=2), jnp.sum(torque_b, axis=2)], axis=1)
    return (on_a, on_b)


def block_pass(fetch, live, width):
    total = live.shape[0]
    slot_ids = jnp.arange(total, dtype=jnp.int32)
    order = jnp.argsort(jnp.where(live, slot_ids, slot_ids + total))
    live_total = jnp.sum(live.astype(jnp.int32))
    empty = jnp.zeros((total, 6, width), jnp.float32)

    def group_step(group, carry):
        out_a, out_b = carry
        first = group * GROUP
        ids = lax.dynamic_slice_in_dim(order, first, GROUP, 0)
        keep = (first + jnp.arange(GROUP) < live_total)[:, None, None]
        left, right = fetch(ids)
        on_a, on_b = pair_forces(left, right)
        out_a = out_a.at[ids].add(jnp.where(keep, on_a, 0.0))
        out_b = out_b.at[ids].add(jnp.where(keep, on_b, 0.0))
        return (out_a, out_b)

    return lax.fori_loop(0, (live_total + GROUP - 1) // GROUP, group_step, (empty, empty))


def body(segments, ship_list, kept_tiles, kept_count, lent_tiles, lent_count):
    leaves = segments.shape[0]
    width = segments.shape[2]
    bricks = lax.axis_size("brick")
    slots = ship_list.shape[2]
    shipped = ship_list[0].reshape(-1)
    outgoing = segments[shipped].reshape(bricks, slots, 8, width)
    incoming = lax.all_to_all(outgoing, "brick", split_axis=0, concat_axis=0, tiled=True)
    extended = jnp.concatenate([segments, incoming.reshape(bricks * slots, 8, width)], axis=0)
    totals = jnp.zeros((extended.shape[0], 6, width), jnp.float32)
    count = kept_count[0]
    kept_ids = kept_tiles[0]

    def kept_step(group, acc):
        first = group * GROUP
        ids = lax.dynamic_slice_in_dim(kept_ids, first, GROUP, 0)
        keep = (first + jnp.arange(GROUP) < count)[:, None, None]
        on_a, on_b = pair_forces(extended[ids[:, 0]], extended[ids[:, 1]])
        acc = acc.at[ids[:, 0]].add(jnp.where(keep, on_a, 0.0))
        return acc.at[ids[:, 1]].add(jnp.where(keep, on_b, 0.0))

    totals = lax.fori_loop(0, (count + GROUP - 1) // GROUP, kept_step, totals)
    me = lax.axis_index("region")
    plan = lent_count[0]
    lent_ids = lent_tiles[0]
    lend = lent_ids.shape[1]
    leaving = lax.dynamic_index_in_dim(plan, me, 0, keepdims=False)
    live = (jnp.arange(lend)[None, :] < leaving[:, None]).reshape(-1)
    flat_ids = lent_ids.reshape(-1, 2)

    def fetch_local(ids):
        return (extended[flat_ids[ids, 0]], extended[flat_ids[ids, 1]])

    on_a, on_b = block_pass(fetch_local, live, width)
    totals = totals.at[flat_ids[:, 0]].add(on_a).at[flat_ids[:, 1]].add(on_b)
    ghost_part = totals[leaves:].reshape(bricks, slots, 6, width)
    back = lax.all_to_all(ghost_part, "brick", split_axis=0, concat_axis=0, tiled=True)
    return totals[:leaves].at[shipped].add(back.reshape(-1, 6, width))


def solution(mesh):
    placed = (
        P(("brick", "region"), None, None),
        P(("brick", "region"), None, None),
        P(("brick", "region"), None, None),
        P(("brick", "region")),
        P(("brick", "region"), None, None, None),
        P("brick", None, None),
    )
    return jax.shard_map(
        body,
        mesh=mesh,
        in_specs=placed,
        out_specs=P(("brick", "region"), None, None),
        check_vma=False,
    )
```

profile of v0, /device:TPU:24, one launch (start us, length us, event | category | flops | bytes accessed | tf_op | source)
XLA Modules:
  0.0 207.3 jit_solution(14890953258567160296)
XLA Ops:
  0.9 2.3 %gather_fusion.6 = f32[128,8,128]{2,1,0:T(8,128)} fusion(f32[32,8,128]{2,1,0:T(8,128)} %param.10, s32[1024]{0:T(1024)S(1)} %pad_clamp_fusion.4), kind=kCustom, calls=%fused_computation.6 | custom fusion | bytes 1049088 | tf_op jit(solution)/shard_map/gather | solution.py:88
  3.3 11.3 %all-to-all-start = ((f32[32,4,8,128]{3,2,1,0:T(8,128)}), f32[32,4,8,128]{3,2,1,0:T(8,128)S(1)}, u32[]{:S(2)}, u32[]{:S(2)}) async-start(f32[32,4,8,128]{3,2,1,0:T(8,128)} %bitcast.17), calls=%async_computation | async-start | bytes 1048576 | tf_op jit(solution)/shard_map/all_to_all | solution.py:89
  16.9 2.0 sort.17
  18.9 12.6 %all-to-all-done = f32[32,4,8,128]{3,2,1,0:T(8,128)S(1)} async-done(((f32[32,4,8,128]{3,2,1,0:T(8,128)}), f32[32,4,8,128]{3,2,1,0:T(8,128)S(1)}, u32[]{:S(2)}, u32[]{:S(2)}) %all-to-all-start) | async-done | bytes 524320 | tf_op jit(solution)/shard_map/all_to_all | solution.py:89
  31.6 56.7 %while.29 = (s32[]{:T(128)}, f32[64,6,128]{2,1,0:T(8,128)S(1)}, f32[64,6,128]{2,1,0:T(8,128)S(1)}, s32[]{:T(128)}, s32[64]{0:T(128)S(1)}, /*index=5*/s32[]{:T(12...) while((s32[]{:T(128)}, f32[64,6,128]{2,1,0:T(8,128)S(1)}, ...), condition=%wide.region_29.30_spmd, body=%wide.region_16.29_spmd.sunk | while | flops 18392196 | bytes 33305504 | solution.py:79
  34.9 1.1 fusion.67
  38.4 1.1 fusion.71
  46.2 1.1 fusion.67
  49.8 1.1 fusion.71
  57.5 1.1 fusion.67
  61.1 1.1 fusion.71
  68.9 1.1 fusion.67
  72.4 1.1 fusion.71
  83.8 1.1 fusion.71
  88.3 20.4 %while.28 = (s32[]{:T(128)}, f32[160,6,128]{2,1,0:T(8,128)S(1)}, s32[]{:T(128)}, s32[64,2]{0,1:T(2,128)S(1)}, s32[]{:T(128)}, /*index=5*/f32[160,8,128]{2,1,0:T(...) while((s32[]{:T(128)}, f32[160,6,128]{2,1,0:T(8,128)S(1)}, s32[]{:T(128)}, s32[64,2]{0,1:T(2,128)S(1)}, ...), condition=%wide.region_13.14_spmd, body=%wide.region_0.13_spmd.sunk | while | flops 18392132 | bytes 33305200 | solution.py:103
  90.3 1.1 fusion.59
  93.9 1.1 fusion.63
  100.4 1.1 fusion.59
  104.0 1.1 fusion.63
  108.7 2.7 %scatter_fusion.4 = f32[160,6,128]{2,1,0:T(8,128)S(1)} fusion(f32[160,6,128]{2,1,0:T(8,128)S(1)} %get-tuple-element.233, s32[64]{0:T(128)S(1)} %get-tuple-element.337, f32[64,6,128]{2,1,0:T(8,128)S(1)} %get-tuple-element.235), kind=kCustom, calls=%fused_computation.11 | custom fusion | flops 49152 | bytes 590080 | tf_op jit(solution)/shard_map/scatter-add | solution.py:116
  111.4 2.7 %scatter_fusion.5 = f32[160,6,128]{2,1,0:T(8,128)S(1)} fusion(f32[160,6,128]{2,1,0:T(8,128)S(1)} %scatter_fusion.4, s32[64]{0:T(128)S(1)} %get-tuple-element.336, f32[64,6,128]{2,1,0:T(8,128)S(1)} %get-tuple-element.236), kind=kCustom, calls=%fused_computation.12 | custom fusion | flops 49152 | bytes 590080 | tf_op jit(solution)/shard_map/scatter-add | solution.py:116
  115.1 74.9 %all-to-all-start.1 = ((f32[32,4,6,128]{3,1,2,0:T(4,128)}), f32[32,4,6,128]{3,1,2,0:T(4,128)S(1)}, u32[]{:S(2)}, u32[]{:S(2)}) async-start(f32[32,4,6,128]{3,1,2,0:T(4,128)} %copy.27), calls=%async_computation.1 | async-start | bytes 786432 | tf_op jit(solution)/shard_map/all_to_all | solution.py:118
  189.9 11.4 %all-to-all-done.1 = f32[32,4,6,128]{3,1,2,0:T(4,128)S(1)} async-done(((f32[32,4,6,128]{3,1,2,0:T(4,128)}), f32[32,4,6,128]{3,1,2,0:T(4,128)S(1)}, u32[]{:S(2)}, u32[]{:S(2)}) %all-to-all-start.1) | async-done | bytes 393248 | tf_op jit(solution)/shard_map/all_to_all | solution.py:118
  201.6 5.0 %scatter_fusion.6 = f32[32,6,128]{2,1,0:T(8,128)S(1)} fusion(f32[32,6,128]{2,1,0:T(8,128)S(1)} %slice.390, s32[128]{0:T(128)S(1)} %fusion.26, f32[128,6,128]{2,1,0:T(8,128)S(1)} %copy.29), kind=kCustom, calls=%fused_computation.13 | custom fusion | flops 98304 | bytes 1180160 | tf_op jit(solution)/shard_map/scatter-add | solution.py:119
  (227 shorter events, 65.3 us)
Async XLA Ops:
  0.0 15.3 %copy-start = (s32[1,8,8]{2,1,0:T(8,128)S(1)}, s32[1,8,8]{2,1,0:T(8,128)}, u32[]{:S(2)}) copy-start(s32[1,8,8]{2,1,0:T(8,128)} %param.15) | copy-start | bytes 772
  0.0 31.5 %copy-start.1 = (f32[32,8,128]{2,1,0:T(8,128)S(1)}, f32[32,8,128]{2,1,0:T(8,128)}, u32[]{:S(2)}) copy-start(f32[32,8,128]{2,1,0:T(8,128)} %param.10) | copy-start | bytes 393220
  0.0 16.8 %copy-start.3 = (s32[1,8,8,2]{2,3,1,0:T(2,128)S(1)}, s32[1,8,8,2]{2,3,1,0:T(2,128)}, u32[]{:S(2)}) copy-start(s32[1,8,8,2]{2,3,1,0:T(2,128)} %param.14) | copy-start | bytes 1540
  3.3 28.2 %all-to-all-start = ((f32[32,4,8,128]{3,2,1,0:T(8,128)}), f32[32,4,8,128]{3,2,1,0:T(8,128)S(1)}, u32[]{:S(2)}, u32[]{:S(2)}) async-start(f32[32,4,8,128]{3,2,1,0:T(8,128)} %bitcast.17), calls=%async_computation | async-start | bytes 1048576 | tf_op jit(solution)/shard_map/all_to_all | solution.py:89
  31.6 56.7 %copy-start.2 = (s32[1,64,2]{1,2,0:T(2,128)S(1)}, s32[1,64,2]{1,2,0:T(2,128)}, u32[]{:S(2)}) copy-start(s32[1,64,2]{1,2,0:T(2,128)} %param.12) | copy-start | bytes 1540
  115.1 86.3 %all-to-all-start.1 = ((f32[32,4,6,128]{3,1,2,0:T(4,128)}), f32[32,4,6,128]{3,1,2,0:T(4,128)S(1)}, u32[]{:S(2)}, u32[]{:S(2)}) async-start(f32[32,4,6,128]{3,1,2,0:T(4,128)} %copy.27), calls=%async_computation.1 | async-start | bytes 786432 | tf_op jit(solution)/shard_map/all_to_all | solution.py:118
where the time goes:
time: 209 us; the launch traced here: 207 us
  starting transfers between devices  86.2 us (41%)
  other arithmetic  74.2 us (36%)
  waiting for transfers between devices  23.9 us (11%)
  local copies, waits for them, and re-layouts  20 us (10%)
    all_to_all x1, starting transfers between devices, body(): lax.all_to_all(ghost_part, 'brick', split_axis=0, concat_axis=0, tiled=True)  74.9 us
    all_to_all x1, waiting for transfers between devices, body(): lax.all_to_all(outgoing, 'brick', split_axis=0, concat_axis=0, tiled=True)  12.6 us
    gather x20, local copies, waits for them, and re-layouts, fetch_local(): return (extended[flat_ids[ids, 0]], extended[flat_ids[ids, 1]])  12.1 us
    all_to_all x1, waiting for transfers between devices, body(): lax.all_to_all(ghost_part, 'brick', split_axis=0, concat_axis=0, tiled=True)  11.4 us
    all_to_all x1, starting transfers between devices, body(): lax.all_to_all(outgoing, 'brick', split_axis=0, concat_axis=0, tiled=True)  11.3 us
    neg x7, other arithmetic, pair_forces(): torque_b = cross_rows((param_b - 0.5)[:, None] * axis_b, -force)  7.62 us
    reduce_sum x7, other arithmetic, pair_forces(): proj_b = jnp.sum(axis_b * offset, axis=1)  7.6 us
    reduce_sum x7, other arithmetic, pair_forces(): dist = jnp.sqrt(jnp.maximum(jnp.sum(gap * gap, axis=1), DIST_FLOOR))  7.05 us
  transfers between devices with their start and end apart: 2, of which 2 were waited for; matrix products, arithmetic and copies ran while one was open for 1% of the time, Pallas kernels for 0%

commit v1 on v0

v1 whole, which is shorter than its diff:
```python
import functools
import jax, jax.numpy as jnp
from jax import lax
from jax.experimental import pallas as pl
from jax.experimental.pallas import tpu as pltpu
from jax.sharding import PartitionSpec as P

MESH = pl.DeviceIdType.MESH
F32, BF16 = jnp.float32, jnp.bfloat16
DIST_FLOOR = 0.0025
PARALLEL_FLOOR = 0.05
TINY = 1e-20
DEPTH = 80

def split3(x):
    hi = x.astype(BF16).astype(F32)
    rest = x - hi
    mid = rest.astype(BF16).astype(F32)
    return hi, mid, rest - mid

def rowsum(x, first, last):
    row = lax.broadcasted_iota(jnp.int32, x.shape, 0)
    return jnp.sum(jnp.where((row >= first) & (row < last), x, 0.0), axis=0, keepdims=True)

def prepare(seg, origin, feat, left, right, blk):
    p = seg[0:3] - origin
    d = seg[3:6]
    a = jnp.sum(d * d, axis=0, keepdims=True)
    inv = lax.rsqrt(a)
    u = d * inv
    length = a * inv
    along = jnp.sum(u * p, axis=0, keepdims=True)
    r = seg[6:7]
    ir = 1.0 / r
    ie = 0.75 / seg[7:8]
    one = jnp.ones_like(r)
    x1 = jnp.concatenate([u, p, along, one], axis=0)
    x2 = jnp.concatenate([length, r, ir, ie, jnp.zeros((4, 128), F32)], axis=0)
    feat[blk, 0:8, :] = x1
    feat[blk, 8:16, :] = x2
    h1, m1, l1 = split3(x1)
    h2, m2, l2 = split3(x2)
    rows = jnp.concatenate([h1, h1, m1, m1, h1, l1, h2, m2, l2, jnp.zeros((128 - 72, 128), F32)], axis=0)
    left[blk] = rows.T.astype(BF16)
    z = jnp.zeros((3, 128), F32)
    z1 = jnp.zeros((1, 128), F32)
    for q, part in enumerate((
        jnp.concatenate([u, z, z1, z1], axis=0),
        jnp.concatenate([-p, z, one, z1], axis=0),
        jnp.concatenate([z, u, z1, -along], axis=0),
    )):
        h, m, l = split3(part)
        right[blk, :, 128 * q:128 * q + 128] = jnp.concatenate([h, m, h, m, l, h], axis=0).astype(BF16)

def spread_matrix():
    row = lax.broadcasted_iota(jnp.int32, (128, 128), 0)
    cols = []
    for q in range(6):
        cols.append((row == q) | (row == 16 + q) | (row == 40 + q))
    for q in range(4):
        cols.append((row == 48 + q) | (row == 56 + q) | (row == 64 + q))
    return jnp.concatenate([jnp.where(c, 1.0, 0.0) for c in cols], axis=1).astype(BF16)

def products(a, b, left, right, spread, dots, wide):
    lhs = left[a]
    dots[...] = jnp.dot(lhs[:, 0:48], right[b], preferred_element_type=F32)
    wide[...] = jnp.dot(lhs, spread[...], preferred_element_type=F32)

def tile(b, feat, dots, wide, cols):
    def lane(q):
        return jnp.broadcast_to(feat[b, q:q + 1, :], (8, 128))
    u2 = [lane(q) for q in range(3)]
    p2 = [lane(3 + q) for q in range(3)]
    len2, r2, ir2, ie2 = [lane(8 + q) for q in range(4)]
    fsum = [None] * 6
    for g in range(16):
        rs = slice(8 * g, 8 * g + 8)
        w, c, f = [dots[rs, 128 * q:128 * q + 128] for q in range(3)]
        wd = [wide[rs, 128 * q:128 * q + 128] for q in range(10)]
        u1, p1 = wd[0:3], wd[3:6]
        len1, r1, ir1, ie1 = wd[6:10]
        den = jnp.maximum(1.0 - w * w, PARALLEL_FLOOR)
        s = (w * f - c) * pltpu.reciprocal(den, approx=True)
        s = jnp.minimum(jnp.maximum(s, 0.0), len1)
        t = jnp.minimum(jnp.maximum(w * s + f, 0.0), len2)
        s = jnp.minimum(jnp.maximum(w * t - c, 0.0), len1)
        gap = [(p1[q] - p2[q]) + s * u1[q] - t * u2[q] for q in range(3)]
        m = jnp.maximum(gap[0] * gap[0] + gap[1] * gap[1] + gap[2] * gap[2], DIST_FLOOR)
        y = lax.rsqrt(m)
        h = jnp.maximum(r1 + r2 - m * y, TINY)
        k = (h * h) * (lax.rsqrt(h * (ir1 + ir2)) * y) * pltpu.reciprocal(ie1 + ie2, approx=True)
        force = [k * x for x in gap]
        vals = force + [s * x for x in force]
        for q in range(6):
            cols[rs, q:q + 1] = jnp.sum(vals[q], axis=1, keepdims=True)
        back = force + [t * x for x in force]
        for q in range(6):
            fsum[q] = back[q] if g == 0 else fsum[q] + back[q]
    on_a = cols[...].T[0:8]
    on_b = -jnp.concatenate([jnp.sum(x, axis=0, keepdims=True) for x in fsum], axis=0)
    return on_a, on_b


def greet(bricks):
    me = lax.axis_index("brick")
    barrier = pltpu.get_barrier_semaphore()
    for off in range(1, bricks):
        pl.semaphore_signal(barrier, inc=1, device_id={"brick": lax.rem(me + off, bricks)}, device_id_type=MESH)
    return me, barrier

def send_kernel(bricks, slots, seg, ship, ext, stage, send_sem, recv_sem):
    me, barrier = greet(bricks)
    leaves = seg.shape[0]
    ext[0:leaves] = seg[...]
    for q in range(bricks):
        for k in range(slots):
            stage[q * slots + k] = seg[ship[q * slots + k]]
    pl.semaphore_wait(barrier, bricks - 1)
    mine = ext.at[pl.ds(leaves + me * slots, slots)]
    for off in range(1, bricks):
        q = lax.rem(me + off, bricks)
        pltpu.make_async_remote_copy(
            src_ref=stage.at[pl.ds(q * slots, slots)], dst_ref=mine, send_sem=send_sem, recv_sem=recv_sem,
            device_id={"brick": q}, device_id_type=MESH).start()
    ext[pl.ds(leaves + me * slots, slots)] = stage[pl.ds(me * slots, slots)]
    total = (bricks - 1) * slots
    pltpu.make_async_copy(stage.at[0:total], ext.at[0:total], recv_sem).wait()
    pltpu.make_async_copy(stage.at[0:total], ext.at[0:total], send_sem).wait()

def back_kernel(bricks, slots, ghosts, back, send_sem, recv_sem):
    me, barrier = greet(bricks)
    pl.semaphore_wait(barrier, bricks - 1)
    rows = 6 * slots
    for off in range(1, bricks):
        q = lax.rem(me + off, bricks)
        pltpu.make_async_remote_copy(
            src_ref=ghosts.at[q], dst_ref=back.at[me], send_sem=send_sem, recv_sem=recv_sem,
            device_id={"brick": q}, device_id_type=MESH).start()
    back[me] = ghosts[me]
    pltpu.make_async_copy(ghosts.at[0:bricks - 1], back.at[0:bricks - 1], recv_sem).wait()
    pltpu.make_async_copy(ghosts.at[0:bricks - 1], back.at[0:bricks - 1], send_sem).wait()

def tile_kernel(leaves, seg, kept, kept_count, lent, plan, own, ghosts, ids_a, ids_b, acc, feat, left, right, spread,
                dots0, dots1, wide0, wide1, cols0, cols1):
    blocks = seg.shape[0]
    region = lax.axis_index("region")
    origin = jnp.broadcast_to(seg[0, 0:3, 0:1], (3, 128))
    spread[...] = spread_matrix()
    acc[...] = jnp.zeros_like(acc)
    cols0[...] = jnp.zeros_like(cols0)
    cols1[...] = jnp.zeros_like(cols1)
    UN = 4
    def prep(i, _):
        for k in range(UN):
            prepare(seg[i * UN + k], origin, feat, left, right, i * UN + k)
        return 0
    lax.fori_loop(0, blocks // UN, prep, 0)

    n_kept = kept_count[0]
    def list_kept(i, _):
        ids_a[i] = kept[2 * i]
        ids_b[i] = kept[2 * i + 1]
        return 0
    lax.fori_loop(0, n_kept, list_kept, 0)
    regions = plan.shape[1]
    lend = lent.shape[0] // (2 * regions)
    n = n_kept
    for j in range(regions):
        live = plan[region, j]
        def list_lent(i, n, j=j):
            ids_a[n + i] = lent[2 * (j * lend + i)]
            ids_b[n + i] = lent[2 * (j * lend + i) + 1]
            return n
        lax.fori_loop(0, live, list_lent, n)
        n = n + live

    last = n - 1
    def at(t):
        t = jnp.minimum(t, last)
        return ids_a[t], ids_b[t]
    a, b = at(0)
    products(a, b, left, right, spread, dots0, wide0)
    def step(i, _):
        a0, b0 = at(2 * i)
        a1, b1 = at(2 * i + 1)
        products(a1, b1, left, right, spread, dots1, wide1)
        x, y = tile(b0, feat, dots0, wide0, cols0)
        acc[a0, 0:6] += x[0:6]
        acc[b0, 0:6] += y
        a2, b2 = at(2 * i + 2)
        products(a2, b2, left, right, spread, dots0, wide0)
        x, y = tile(b1, feat, dots1, wide1, cols1)
        live = 2 * i + 1 < n
        acc[a1, 0:6] += jnp.where(live, x[0:6], 0.0)
        acc[b1, 0:6] += jnp.where(live, y, 0.0)
        return 0
    lax.fori_loop(0, (n + 1) // 2, step, 0)
    own[...] = acc[0:leaves]
    bricks, rows, _ = ghosts.shape
    slots = rows // 6
    for q in range(bricks):
        for k in range(slots):
            ghosts[q, 6 * k:6 * k + 6] = acc[leaves + q * slots + k, 0:6]

def finish_kernel(slots, seg, ship, own, back, out, acc0, acc1, acc2, acc3):
    accs = (acc0, acc1, acc2, acc3)
    acc0[...] = own[...]
    for acc in accs[1:]:
        acc[...] = jnp.zeros_like(acc)
    bricks = back.shape[0]
    for q in range(bricks):
        for k in range(slots):
            acc = accs[k % 4]
            leaf = ship[q * slots + k]
            acc[leaf, 0:6] += back[q, 6 * k:6 * k + 6]
    for i in range(seg.shape[0]):
        total = acc0[i] + acc1[i] + acc2[i] + acc3[i]
        d = [seg[i, 3 + q:4 + q] for q in range(3)]
        a = d[0] * d[0] + d[1] * d[1] + d[2] * d[2]
        inv = lax.rsqrt(a)
        half = 0.5 * (a * inv)
        u = [x * inv for x in d]
        force = [total[q:q + 1] for q in range(3)]
        lever = [total[3 + q:4 + q] - half * force[q] for q in range(3)]
        torque = [u[(q + 1) % 3] * lever[(q + 2) % 3] - u[(q + 2) % 3] * lever[(q + 1) % 3] for q in range(3)]
        out[i] = jnp.concatenate(force + torque, axis=0)

VM = pl.BlockSpec(memory_space=pltpu.VMEM)
SM = pl.BlockSpec(memory_space=pltpu.SMEM)

def body(segments, ship_list, kept_tiles, kept_count, lent_tiles, lent_count):
    leaves, _, width = segments.shape
    bricks = lax.axis_size("brick")
    slots = ship_list.shape[2]
    ghosts = bricks * slots
    blocks = leaves + ghosts
    shape = lambda *s: jax.ShapeDtypeStruct(s, F32)
    ship = ship_list.reshape(-1)
    kept = kept_tiles.reshape(-1)
    lent = lent_tiles.reshape(-1)
    limit = 48 * 2**20
    ext = pl.pallas_call(
        functools.partial(send_kernel, bricks, slots),
        out_shape=shape(blocks, 8, width),
        in_specs=[VM, SM], out_specs=VM,
        scratch_shapes=[pltpu.VMEM((ghosts, 8, width), F32), pltpu.SemaphoreType.DMA, pltpu.SemaphoreType.DMA],
        compiler_params=pltpu.CompilerParams(collective_id=0, has_side_effects=True, vmem_limit_bytes=limit),
    )(segments, ship)
    slots_total = kept.shape[0] // 2 + lent.shape[0] // 2
    own, part = pl.pallas_call(
        functools.partial(tile_kernel, leaves),
        out_shape=(shape(leaves, 8, width), shape(bricks, 6 * slots, width)),
        in_specs=[VM, SM, SM, SM, SM], out_specs=(VM, VM),
        scratch_shapes=[
            pltpu.SMEM((slots_total,), jnp.int32), pltpu.SMEM((slots_total,), jnp.int32),
            pltpu.VMEM((blocks, 8, 128), F32),
            pltpu.VMEM((blocks, 16, 128), F32),
            pltpu.VMEM((blocks, 128, 128), BF16),
            pltpu.VMEM((blocks, 48, 384), BF16),
            pltpu.VMEM((128, 1280), BF16),
            pltpu.VMEM((128, 384), F32), pltpu.VMEM((128, 384), F32),
            pltpu.VMEM((128, 1280), F32), pltpu.VMEM((128, 1280), F32),
            pltpu.VMEM((128, 128), F32), pltpu.VMEM((128, 128), F32),
        ],
        compiler_params=pltpu.CompilerParams(vmem_limit_bytes=limit),
    )(ext, kept, kept_count, lent, lent_count[0])
    back = pl.pallas_call(
        functools.partial(back_kernel, bricks, slots),
        out_shape=shape(bricks, 6 * slots, width),
        in_specs=[VM], out_specs=VM,
        scratch_shapes=[pltpu.SemaphoreType.DMA, pltpu.SemaphoreType.DMA],
        compiler_params=pltpu.CompilerParams(collective_id=1, has_side_effects=True, vmem_limit_bytes=limit),
    )(part)
    return pl.pallas_call(
        functools.partial(finish_kernel, slots),
        out_shape=shape(leaves, 6, width),
        in_specs=[VM, SM, VM, VM], out_specs=VM,
        scratch_shapes=[pltpu.VMEM((leaves, 8, width), F32)] * 4,
        compiler_params=pltpu.CompilerParams(vmem_limit_bytes=limit),
    )(segments, ship, own, back)

def solution(mesh):
    placed = (
        P(("brick", "region"), None, None),
        P(("brick", "region"), None, None),
        P(("brick", "region"), None, None),
        P(("brick", "region")),
        P(("brick", "region"), None, None, None),
        P("brick", None, None),
    )
    return jax.shard_map(body, mesh=mesh, in_specs=placed, out_specs=P(("brick", "region"), None, None), check_vma=False)
```

time: 209 us -> 82.1 us (0.39)
  starting transfers between devices: 86.2 us -> 0 us
  Pallas kernels: 0 us -> 77.8 us
  other arithmetic: 74.2 us -> 0 us
  waiting for transfers between devices: 23.9 us -> 0 us
  local copies, waits for them, and re-layouts: 20 us -> 3.4 us
    all_to_all x2 -> x0, starting transfers between devices: 86.2 us -> none  [the longest x1 74.9 us: body(): lax.all_to_all(ghost_part, 'brick', split_axis=0, concat_axis=0, tiled=True)]
    pallas_call x0 -> x4, Pallas kernels: none -> 77.8 us  [the longest x1 34 us: body(): pl.pallas_call(functools.partial(back_kernel, bricks, slots), out_shape=s...]
    all_to_all x2 -> x0, waiting for transfers between devices: 23.9 us -> none  [the longest x1 12.6 us: body(): lax.all_to_all(outgoing, 'brick', split_axis=0, concat_axis=0, tiled=True)]
    reduce_sum x43 -> x0, other arithmetic: 23.5 us -> none  [the longest x7 7.6 us: pair_forces(): proj_b = jnp.sum(axis_b * offset, axis=1)]
    scatter-add x17 -> x0, other arithmetic: 21.3 us -> none  [the longest x2 5.46 us: body(): totals = totals.at[flat_ids[:, 0]].add(on_a).at[flat_ids[:, 1]].add(on_b)]
    gather x25 -> x0, local copies, waits for them, and re-layouts: 16.6 us -> none  [the longest x20 12.1 us: fetch_local(): return (extended[flat_ids[ids, 0]], extended[flat_ids[ids, 1]])]
    sub x28 -> x0, other arithmetic: 9.37 us -> none  [the longest x14 3.98 us: cross_rows(): lever[:, 1] * force[:, 2] - lever[:, 2] * force[:, 1]]
    neg x14 -> x0, other arithmetic: 7.66 us -> none  [the longest x7 7.62 us: pair_forces(): torque_b = cross_rows((param_b - 0.5)[:, None] * axis_b, -force)]
  transfers between devices with their start and end apart: 2 -> 0, of which waited for: 2 -> 0; matrix products, arithmetic and copies ran while one was open for 1% -> 0% of each run, Pallas kernels for 0% -> 0%
where the time goes in v1:
time: 82.1 us; the launch traced here: 81.9 us
  Pallas kernels  77.8 us (95%)
  local copies, waits for them, and re-layouts  3.4 us (4%)
    pallas_call x1, Pallas kernels, body(): pl.pallas_call(functools.partial(back_kernel, bricks, slots), out_shape=s...  34 us
    pallas_call x1, Pallas kernels, body(): pl.pallas_call(functools.partial(send_kernel, bricks, slots), out_shape=s...  23.2 us
    pallas_call x1, Pallas kernels, body(): pl.pallas_call(functools.partial(tile_kernel, leaves), out_shape=(shape(l...  19.7 us
    unnamed x7, local copies, waits for them, and re-layouts  2.36 us

profile of v1, /device:TPU:24, one launch (start us, length us, event | category | flops | bytes accessed | tf_op | source)
XLA Modules:
  0.0 81.9 jit_solution(10648470799004497954)
XLA Ops:
  0.0 0.0 copy-start
  0.7 0.8 copy.11
  1.5 0.1 reshape.9.ship
  1.6 0.8 copy.12
  2.3 0.1 reshape.10.kept
  2.5 0.8 copy.13
  3.3 0.1 reshape.11.lent
  3.4 0.0 copy-done
  3.4 0.0 copy-start.1
  3.4 23.2 %shard_map.64.seg = f32[160,8,128]{2,1,0:T(8,128)S(1)} custom-call(f32[32,8,128]{2,1,0:T(8,128)S(1)} %copy-done, s32[128]{0:T(128)S(1)} %reshape.9.ship), custom_call_target="tpu_custom_call" | custom-call | tf_op jit(solution)/shard_map/pallas_call | solution.py:242
  26.7 0.0 copy-done.1
  26.7 19.7 %shard_map.65 = (f32[32,8,128]{2,1,0:T(8,128)S(1)}, f32[32,24,128]{2,1,0:T(8,128)S(1)}) custom-call(f32[160,8,128]{2,1,0:T(8,128)S(1)} %shard_map.64.seg, s32[128]{0:T(128)S(1)} %reshape.10.kept, s32[1]{0:T(128)S(6)} %copy.15.kept_count, s32[128]{0:T(128)S(1)} %reshape.11.lent, s32[8,8]{1,0:T(8,128)S(1)} %bitcast.3), custom_call_target="tpu_custom_call" | custom-call | tf_op jit(solution)/shard_map/pallas_call | solution.py:250
  46.3 34.0 %shard_map.66.back = f32[32,24,128]{2,1,0:T(8,128)S(1)} custom-call(f32[32,24,128]{2,1,0:T(8,128)S(1)} %get-tuple-element.8.ghosts), custom_call_target="tpu_custom_call" | custom-call | tf_op jit(solution)/shard_map/pallas_call | solution.py:267
  80.3 0.9 %shard_map.67 = f32[32,6,128]{2,1,0:T(8,128)S(1)} custom-call(f32[32,8,128]{2,1,0:T(8,128)S(1)} %copy-done, s32[128]{0:T(128)S(1)} %reshape.9.ship, f32[32,8,128]{2,1,0:T(8,128)S(1)} %get-tuple-element.7.own, f32[32,24,128]{2,1,0:T(8,128)S(1)} %shard_map.66.back), custom_call_target="tpu_custom_call" | custom-call | tf_op jit(solution)/shard_map/pallas_call | solution.py:274
  81.3 0.7 copy.14
Async XLA Ops:
  0.0 3.4 %copy-start = (f32[32,8,128]{2,1,0:T(8,128)S(1)}, f32[32,8,128]{2,1,0:T(8,128)}, u32[]{:S(2)}) copy-start(f32[32,8,128]{2,1,0:T(8,128)} %seg.3) | copy-start | bytes 393220
  3.4 23.2 %copy-start.1 = (s32[1,8,8]{2,1,0:T(8,128)S(1)}, s32[1,8,8]{2,1,0:T(8,128)}, u32[]{:S(2)}) copy-start(s32[1,8,8]{2,1,0:T(8,128)} %param.11) | copy-start | bytes 772

commit v2 on v1

v2 whole, which is shorter than its diff:
```python
import functools
import jax, jax.numpy as jnp
from jax import lax
from jax.experimental import pallas as pl
from jax.experimental.pallas import tpu as pltpu
from jax.sharding import PartitionSpec as P

MESH = pl.DeviceIdType.MESH
F32, BF16 = jnp.float32, jnp.bfloat16
DIST_FLOOR = 0.0025
PARALLEL_FLOOR = 0.05
TINY = 1e-20
LARGE = 1e30

def split3(x):
    hi = x.astype(BF16).astype(F32)
    rest = x - hi
    mid = rest.astype(BF16).astype(F32)
    return hi, mid, rest - mid

def prepare(seg, origin, feat, left, right, more, blk):
    p = seg[0:3] - origin
    d = seg[3:6]
    a = jnp.sum(d * d, axis=0, keepdims=True)
    inv = lax.rsqrt(a)
    u = d * inv
    length = a * inv
    along = jnp.sum(u * p, axis=0, keepdims=True)
    r = seg[6:7]
    ir = jnp.minimum(1.0 / r, LARGE)
    ie = jnp.minimum(0.75 / seg[7:8], LARGE)
    one = jnp.ones_like(r)
    x1 = jnp.concatenate([u, p, along, one], axis=0)
    x2 = jnp.concatenate([length, r, ir, ie, jnp.zeros((4, 128), F32)], axis=0)
    feat[blk] = jnp.concatenate([u, length, jnp.zeros((4, 128), F32)], axis=0)
    h1, m1, l1 = split3(x1)
    h2, m2, l2 = split3(x2)
    rows = jnp.concatenate([h1, h1, m1, m1, h1, l1, h2, m2, l2, jnp.ones((8, 128), F32), jnp.zeros((128 - 80, 128), F32)], axis=0)
    left[blk] = rows.T.astype(BF16)
    for q, x in enumerate(extra(p, r, ir, ie)):
        more[blk, :, 128 * q:128 * q + 128] = x
    z = jnp.zeros((3, 128), F32)
    z1 = jnp.zeros((1, 128), F32)
    for q, part in enumerate((
        jnp.concatenate([u, z, z1, z1], axis=0),
        jnp.concatenate([-p, z, one, z1], axis=0),
        jnp.concatenate([z, u, z1, -along], axis=0),
    )):
        h, m, l = split3(part)
        right[blk, :, 128 * q:128 * q + 128] = jnp.concatenate([h, m, h, m, l, h], axis=0).astype(BF16)

def extra(p, r, ir, ie):
    row = lax.broadcasted_iota(jnp.int32, (8, 128), 0)
    out = []
    for keep, x in ((-1, -p[0:1]), (-1, -p[1:2]), (-1, -p[2:3]), (1, r), (2, ir), (3, ie)):
        h, m, l = split3(x)
        out.append(jnp.concatenate([jnp.where(row == keep, 1.0, 0.0), h, m, l, jnp.zeros((5, 128), F32)], axis=0).astype(BF16))
    return out

def spread_matrix():
    row = lax.broadcasted_iota(jnp.int32, (128, 128), 0)
    cols = []
    for q in range(6):
        cols.append((row == q) | (row == 16 + q) | (row == 40 + q))
    for q in range(4):
        cols.append((row == 48 + q) | (row == 56 + q) | (row == 64 + q))
    return jnp.concatenate([jnp.where(c, 1.0, 0.0) for c in cols], axis=1).astype(BF16)

def products(a, b, left, right, more, spread, dots, wide):
    lhs = left[a]
    spread[64:80, 384:768] = more[b, :, 0:384]
    spread[64:80, 896:1280] = more[b, :, 384:768]
    dots[...] = jnp.dot(lhs[:, 0:48], right[b], preferred_element_type=F32)
    wide[...] = jnp.dot(lhs[:, 0:80], spread[0:80], preferred_element_type=F32)

def tile(b, feat, dots, wide, diag):
    def lane(q):
        return jnp.broadcast_to(feat[b, q:q + 1, :], (8, 128))
    u2 = [lane(q) for q in range(3)]
    len2 = lane(3)
    fsum = [None] * 6
    asum = [None] * 6
    for g in range(16):
        rs = slice(8 * g, 8 * g + 8)
        w, c, f = [dots[rs, 128 * q:128 * q + 128] for q in range(3)]
        wd = [wide[rs, 128 * q:128 * q + 128] for q in range(10)]
        u1, apart = wd[0:3], wd[3:6]
        len1, reach, ir, ie = wd[6:10]
        den = jnp.maximum(1.0 - w * w, PARALLEL_FLOOR)
        s = (w * f - c) * pltpu.reciprocal(den, approx=True)
        s = jnp.minimum(jnp.maximum(s, 0.0), len1)
        t = jnp.minimum(jnp.maximum(w * s + f, 0.0), len2)
        s = jnp.minimum(jnp.maximum(w * t - c, 0.0), len1)
        gap = [apart[q] + s * u1[q] - t * u2[q] for q in range(3)]
        m = jnp.maximum(gap[0] * gap[0] + gap[1] * gap[1] + gap[2] * gap[2], DIST_FLOOR)
        y = lax.rsqrt(m)
        h = jnp.maximum(reach - m * y, TINY)
        k = (h * h) * (lax.rsqrt(h * ir) * y) * pltpu.reciprocal(ie, approx=True)
        force = [k * x for x in gap]
        vals = force + [s * x for x in force]
        if g < 15:
            for q in range(6):
                red = jnp.sum(vals[q], axis=1, keepdims=True)
                asum[q] = jnp.where(diag == g, red, 0.0 if g == 0 else asum[q])
        back = force + [t * x for x in force]
        for q in range(6):
            fsum[q] = back[q] if g == 0 else fsum[q] + back[q]
    return vals + asum + fsum

def settle(pending, diag, acc, a, b, live):
    vals, asum, fsum = pending[0:6], pending[6:12], pending[12:18]
    for q in range(6):
        red = jnp.sum(vals[q], axis=1, keepdims=True)
        asum[q] = jnp.where(diag == 15, red, asum[q])
    on_a = jnp.concatenate([jnp.sum(x, axis=0, keepdims=True) for x in asum], axis=0)
    on_b = jnp.concatenate([jnp.sum(x, axis=0, keepdims=True) for x in fsum], axis=0)
    acc[a, 0:6] += jnp.where(live, on_a, 0.0)
    acc[b, 0:6] -= jnp.where(live, on_b, 0.0)


def greet(bricks):
    me = lax.axis_index("brick")
    barrier = pltpu.get_barrier_semaphore()
    for off in range(1, bricks):
        pl.semaphore_signal(barrier, inc=1, device_id={"brick": lax.rem(me + off, bricks)}, device_id_type=MESH)
    return me, barrier

WAVES = ((0, 0), (1, 7), (2, 6), (3, 5), (4, 4))
NX, NZ = 4, 8

def wave_offsets(wave):
    first, second = WAVES[wave]
    zs = (first,) if first == second else (first, second)
    return [(dx, dz) for dz in zs for dx in range(NX) if (dx, dz) != (0, 0)]

def send_kernel(bricks, slots, seg, ship, feat, left, right, more, ext, stage, send_sem, recv_sems):
    me, barrier = greet(bricks)
    x, z = me // NZ, lax.rem(me, NZ)
    leaves = seg.shape[0]
    for q in range(bricks):
        for k in range(slots):
            stage[q * slots + k] = seg[ship[k, q]]
    origin = jnp.broadcast_to(seg[0, 0:3, 0:1], (3, 128))
    def own(i, _):
        for k in range(4):
            prepare(seg[4 * i + k], origin, feat, left, right, more, 4 * i + k)
        return 0
    lax.fori_loop(0, leaves // 8, own, 0)
    pl.semaphore_wait(barrier, bricks - 1)
    mine = ext.at[pl.ds(me * slots, slots)]
    for wave in range(len(WAVES)):
        for dx, dz in wave_offsets(wave):
            q = lax.rem(x + dx, NX) * NZ + lax.rem(z + dz, NZ)
            pltpu.make_async_remote_copy(
                src_ref=stage.at[pl.ds(q * slots, slots)], dst_ref=mine, send_sem=send_sem, recv_sem=recv_sems.at[wave],
                device_id={"brick": q}, device_id_type=MESH).start()
    lax.fori_loop(leaves // 8, leaves // 4, own, 0)
    def ghosts(q, source):
        for k in range(slots):
            prepare(source[q * slots + k], origin, feat, left, right, more, leaves + q * slots + k)
    ghosts(me, stage)
    for wave in range(len(WAVES)):
        count = len(wave_offsets(wave)) * slots
        pltpu.make_async_copy(stage.at[0:count], ext.at[0:count], recv_sems.at[wave]).wait()
        first, second = WAVES[wave]
        skip = 1 if first == 0 else 0
        def arrived(i, _):
            dz = first + (second - first) * (i // NX)
            q = lax.rem(x + NX - lax.rem(i, NX), NX) * NZ + lax.rem(z + NZ - dz, NZ)
            ghosts(q, ext)
            return 0
        lax.fori_loop(skip, count // slots + skip, arrived, 0)
    total = (bricks - 1) * slots
    pltpu.make_async_copy(stage.at[0:total], ext.at[0:total], send_sem).wait()

def back_kernel(bricks, slots, leaves, acc, back, send_sem, recv_sem):
    me, barrier = greet(bricks)
    rows = slice(0, 6)
    pl.semaphore_wait(barrier, bricks - 1)
    mine = back.at[pl.ds(me * slots, slots), rows]
    for wave in range(len(WAVES)):
        for dx, dz in wave_offsets(wave):
            q = lax.rem(me // NZ + dx, NX) * NZ + lax.rem(me + dz, NZ)
            pltpu.make_async_remote_copy(
                src_ref=acc.at[pl.ds(leaves + q * slots, slots), rows], dst_ref=mine, send_sem=send_sem, recv_sem=recv_sem,
                device_id={"brick": q}, device_id_type=MESH).start()
    back[pl.ds(me * slots, slots)] = acc[pl.ds(leaves + me * slots, slots)]
    total = (bricks - 1) * slots
    pltpu.make_async_copy(acc.at[0:total, rows], back.at[0:total, rows], recv_sem).wait()
    pltpu.make_async_copy(acc.at[0:total, rows], back.at[0:total, rows], send_sem).wait()

def tile_kernel(kept, kept_count, lent, plan, feat, left, right, more, acc, ids_a, ids_b,
                spread0, spread1, dots0, dots1, wide0, wide1, pend):
    region = lax.axis_index("region")
    spread0[...] = spread_matrix()
    spread1[...] = spread_matrix()
    acc[...] = jnp.zeros_like(acc)
    pend[...] = jnp.zeros_like(pend)
    n_kept = kept_count[0]
    def list_kept(i, _):
        ids_a[i] = kept[0, i]
        ids_b[i] = kept[1, i]
        return 0
    lax.fori_loop(0, n_kept, list_kept, 0)
    n = n_kept
    for j in range(plan.shape[1]):
        live = plan[region, j]
        def list_lent(i, first, j=j):
            ids_a[first + i] = lent[j, 0, i]
            ids_b[first + i] = lent[j, 1, i]
            return first
        lax.fori_loop(0, live, list_lent, n)
        n = n + live
    last = n - 1
    def at(t):
        t = jnp.minimum(t, last)
        return ids_a[t], ids_b[t]
    bufs = ((spread0, dots0, wide0), (spread1, dots1, wide1))
    products(*at(0), left, right, more, *bufs[0])
    lanes = lax.broadcasted_iota(jnp.int32, (8, 128), 1)
    diag = jnp.where(lanes % 8 == lax.broadcasted_iota(jnp.int32, (8, 128), 0), lanes // 8, -1)
    def tiles(first, count):
        for k in range(count):
            t = first + k
            a, b = at(t)
            products(*at(t + 1), left, right, more, *bufs[(k + 1) % 2])
            if k == 0:
                pending = [pend[q] for q in range(18)]
                before = at(jnp.maximum(t - 1, 0))
                live = True
            settle(pending, diag, acc, *before, live)
            pending = tile(b, feat, *bufs[k % 2][1:], diag)
            before = (a, b)
            live = t < n
        for q in range(18):
            pend[q] = jnp.where(live, pending[q], 0.0)
    def many(i, _):
        tiles(UNROLL * i, UNROLL)
        return 0
    def few(i, _):
        tiles(2 * i, 2)
        return 0
    whole = n // UNROLL
    lax.fori_loop(0, whole, many, 0)
    pairs = (n + 1) // 2
    lax.fori_loop(whole * (UNROLL // 2), pairs, few, 0)
    settle([pend[q] for q in range(18)], diag, acc, *at(2 * pairs - 1), True)

UNROLL = 4

def finish_kernel(slots, seg, ship, own, back, out, acc0, acc1, acc2, acc3):
    accs = (acc0, acc1, acc2, acc3)
    leaves = seg.shape[0]
    acc0[...] = own[0:leaves]
    for acc in accs[1:]:
        acc[...] = jnp.zeros_like(acc)
    bricks = back.shape[0] // slots
    for q in range(bricks):
        for k in range(slots):
            acc = accs[k % 4]
            leaf = ship[k, q]
            acc[leaf, 0:6] += back[q * slots + k, 0:6]
    for i in range(leaves):
        total = acc0[i] + acc1[i] + acc2[i] + acc3[i]
        d = [seg[i, 3 + q:4 + q] for q in range(3)]
        a = d[0] * d[0] + d[1] * d[1] + d[2] * d[2]
        inv = lax.rsqrt(a)
        half = 0.5 * (a * inv)
        u = [c * inv for c in d]
        force = [total[q:q + 1] for q in range(3)]
        lever = [total[3 + q:4 + q] - half * force[q] for q in range(3)]
        torque = [u[(q + 1) % 3] * lever[(q + 2) % 3] - u[(q + 2) % 3] * lever[(q + 1) % 3] for q in range(3)]
        for q in range(3):
            out[q, i:i + 1] = force[q]
            out[3 + q, i:i + 1] = torque[q]

VM = pl.BlockSpec(memory_space=pltpu.VMEM)
SM = pl.BlockSpec(memory_space=pltpu.SMEM)

def body(segments, ship_list, kept_tiles, kept_count, lent_tiles, lent_count):
    leaves, _, width = segments.shape
    bricks = lax.axis_size("brick")
    slots = ship_list.shape[2]
    ghosts = bricks * slots
    blocks = leaves + ghosts
    def shape(*s, dtype=F32):
        return jax.ShapeDtypeStruct(s, dtype)
    ship = jnp.transpose(ship_list[0], (1, 0))
    kept = jnp.transpose(kept_tiles[0], (1, 0))
    lent = jnp.transpose(lent_tiles[0], (0, 2, 1))
    prepared = pl.pallas_call(
        functools.partial(send_kernel, bricks, slots),
        out_shape=(shape(blocks, 8, width), shape(blocks, 128, 128, dtype=BF16), shape(blocks, 48, 384, dtype=BF16),
                   shape(blocks, 16, 768, dtype=BF16)),
        in_specs=[VM, SM], out_specs=(VM,) * 4,
        scratch_shapes=[pltpu.VMEM((ghosts, 8, width), F32), pltpu.VMEM((ghosts, 8, width), F32),
                        pltpu.SemaphoreType.DMA, pltpu.SemaphoreType.DMA((len(WAVES),))],
        compiler_params=pltpu.CompilerParams(collective_id=0, has_side_effects=True, vmem_limit_bytes=LIMIT),
    )(segments, ship)
    slots_total = kept_tiles.shape[1] + lent_tiles.shape[1] * lent_tiles.shape[2]
    acc = pl.pallas_call(
        tile_kernel,
        out_shape=shape(blocks, 8, width),
        in_specs=[SM] * 4 + [VM] * 4, out_specs=VM,
        scratch_shapes=[
            pltpu.SMEM((slots_total,), jnp.int32), pltpu.SMEM((slots_total,), jnp.int32),
            pltpu.VMEM((128, 1280), BF16), pltpu.VMEM((128, 1280), BF16),
            pltpu.VMEM((128, 384), F32), pltpu.VMEM((128, 384), F32),
            pltpu.VMEM((128, 1280), F32), pltpu.VMEM((128, 1280), F32),
            pltpu.VMEM((18, 8, 128), F32),
        ],
        compiler_params=pltpu.CompilerParams(vmem_limit_bytes=LIMIT),
    )(kept, kept_count, lent, lent_count[0], *prepared)
    back = pl.pallas_call(
        functools.partial(back_kernel, bricks, slots, leaves),
        out_shape=shape(ghosts, 8, width),
        in_specs=[VM], out_specs=VM,
        scratch_shapes=[pltpu.SemaphoreType.DMA, pltpu.SemaphoreType.DMA],
        compiler_params=pltpu.CompilerParams(collective_id=1, has_side_effects=True, vmem_limit_bytes=LIMIT),
    )(acc)
    loads = pl.pallas_call(
        functools.partial(finish_kernel, slots),
        out_shape=shape(6, leaves, width),
        in_specs=[VM, SM, VM, VM], out_specs=VM,
        scratch_shapes=[pltpu.VMEM((leaves, 8, width), F32)] * 4,
        compiler_params=pltpu.CompilerParams(vmem_limit_bytes=LIMIT),
    )(segments, ship, acc, back)
    return jnp.transpose(loads, (1, 0, 2))

LIMIT = 26 * 2**20

def solution(mesh):
    placed = (
        P(("brick", "region"), None, None),
        P(("brick", "region"), None, None),
        P(("brick", "region"), None, None),
        P(("brick", "region")),
        P(("brick", "region"), None, None, None),
        P("brick", None, None),
    )
    return jax.shard_map(body, mesh=mesh, in_specs=placed, out_specs=P(("brick", "region"), None, None), check_vma=False)
```

time: 82.1 us -> 70 us (0.85)
  Pallas kernels: 77.8 us -> 65.4 us
    pallas_call x4, Pallas kernels: 77.8 us -> 65.4 us  [the longest x1 24.3 us: body(): pl.pallas_call(functools.partial(send_kernel, bricks, slots), out_shape=(...]
    unnamed x7 -> x10, local copies, waits for them, and re-layouts: 2.36 us -> 3.64 us
where the time goes in v2:
time: 70 us; the launch traced here: 69.8 us
  Pallas kernels  65.4 us (93%)
  local copies, waits for them, and re-layouts  3.64 us (5%)
    pallas_call x1, Pallas kernels, body(): pl.pallas_call(functools.partial(send_kernel, bricks, slots), out_shape=(...  24.3 us
    pallas_call x1, Pallas kernels, body(): pl.pallas_call(tile_kernel, out_shape=shape(blocks, 8, width), in_specs=[...  21.5 us
    pallas_call x1, Pallas kernels, body(): pl.pallas_call(functools.partial(back_kernel, bricks, slots, leaves), out...  18 us
    unnamed x10, local copies, waits for them, and re-layouts  3.64 us
    pallas_call x1, Pallas kernels, body(): pl.pallas_call(functools.partial(finish_kernel, slots), out_shape=shape(6...  1.56 us

profile of v2, /device:TPU:24, one launch (start us, length us, event | category | flops | bytes accessed | tf_op | source)
XLA Modules:
  0.0 69.8 jit_solution(7538345144071644815)
XLA Ops:
  0.7 0.0 copy-start
  0.7 0.9 %copy-done = f32[32,8,128]{2,1,0:T(8,128)S(1)} copy-done((f32[32,8,128]{2,1,0:T(8,128)S(1)}, f32[32,8,128]{2,1,0:T(8,128)}, u32[]{:S(2)}) %copy-start) | copy-done | bytes 131096
  1.6 0.0 copy-start.2
  1.6 0.7 copy-done.2
  2.2 24.3 %shard_map.64 = (f32[160,8,128]{2,1,0:T(8,128)S(1)}, bf16[160,128,128]{2,1,0:T(8,128)(2,1)S(1)}, bf16[160,48,384]{2,1,0:T(8,128)(2,1)S(1)}, bf16[160,16,768]{2,1,0:T(8,128)(2,1)S(1)}) custom-call(f32[32,8,128]{2,1,0:T(8,128)S(1)} %copy-done, s32[4,32]{1,0:T(4,128)S(1)} %bitcast.12), custom_call_target="tpu_custom_call" | custom-call | tf_op jit(solution)/shard_map/pallas_call | solution.py:291
  26.6 0.0 copy-start.1
  26.6 0.7 copy-done.1
  27.3 0.0 copy-start.3
  27.3 0.7 copy-done.3
  27.9 0.0 copy-start.4
  27.9 0.7 copy-done.4
  28.6 21.5 %shard_map.65.acc.own = f32[160,8,128]{2,1,0:T(8,128)S(1)} custom-call(s32[2,64]{1,0:T(2,128)S(1)} %bitcast.15, s32[1]{0:T(128)S(6)} %copy.10.kept_count, s32[8,2,8]{2,1,0:T(2,128)S(1)} %bitcast.11, s32[8,8]{1,0:T(8,128)S(1)} %bitcast.14, f32[160,8,128]{2,1,0:T(8,128)S(1)} %get-tuple-element.9.feat, bf16[160,128,128]{2,1,0:T(8,128)(2,1)S(1)} %get-tuple-element.10.left, ...), custom_call_target="tpu_custom_call" | custom-call | tf_op jit(solution)/shard_map/pallas_call | solution.py:301
  50.2 18.0 %shard_map.66.back = f32[128,8,128]{2,1,0:T(8,128)S(1)} custom-call(f32[160,8,128]{2,1,0:T(8,128)S(1)} %shard_map.65.acc.own), custom_call_target="tpu_custom_call" | custom-call | tf_op jit(solution)/shard_map/pallas_call | solution.py:314
  68.2 1.6 %shard_map.67 = f32[6,32,128]{2,1,0:T(8,128)} custom-call(f32[32,8,128]{2,1,0:T(8,128)S(1)} %copy-done, s32[4,32]{1,0:T(4,128)S(1)} %bitcast.13, f32[160,8,128]{2,1,0:T(8,128)S(1)} %shard_map.65.acc.own, f32[128,8,128]{2,1,0:T(8,128)S(1)} %shard_map.66.back), custom_call_target="tpu_custom_call" | custom-call | tf_op jit(solution)/shard_map/pallas_call | solution.py:321
Async XLA Ops:
  0.7 0.9 %copy-start = (f32[32,8,128]{2,1,0:T(8,128)S(1)}, f32[32,8,128]{2,1,0:T(8,128)}, u32[]{:S(2)}) copy-start(f32[32,8,128]{2,1,0:T(8,128)} %seg.3) | copy-start | bytes 393220
  1.6 0.7 copy-start.2
  26.6 0.7 %copy-start.1 = (s32[1,8,8,2]{2,3,1,0:T(2,128)S(1)}, s32[1,8,8,2]{2,3,1,0:T(2,128)}, u32[]{:S(2)}) copy-start(s32[1,8,8,2]{2,3,1,0:T(2,128)} %param.10) | copy-start | bytes 1540
  27.3 0.7 copy-start.3
  27.9 0.7 copy-start.4

commit v3 on v2

--- a/solution.py
+++ b/solution.py
@@ -48,6 +48,7 @@
     )):
         h, m, l = split3(part)
         right[blk, :, 128 * q:128 * q + 128] = jnp.concatenate([h, m, h, m, l, h], axis=0).astype(BF16)
+    return u, length
 
 def extra(p, r, ir, ie):
     row = lax.broadcasted_iota(jnp.int32, (8, 128), 0)
@@ -112,10 +113,10 @@
     for q in range(6):
         red = jnp.sum(vals[q], axis=1, keepdims=True)
         asum[q] = jnp.where(diag == 15, red, asum[q])
-    on_a = jnp.concatenate([jnp.sum(x, axis=0, keepdims=True) for x in asum], axis=0)
-    on_b = jnp.concatenate([jnp.sum(x, axis=0, keepdims=True) for x in fsum], axis=0)
-    acc[a, 0:6] += jnp.where(live, on_a, 0.0)
-    acc[b, 0:6] -= jnp.where(live, on_b, 0.0)
+    for q in range(6):
+        acc[q, pl.ds(a, 1), :] += jnp.where(live, jnp.sum(asum[q], axis=0, keepdims=True), 0.0)
+    for q in range(6):
+        acc[q, pl.ds(b, 1), :] -= jnp.where(live, jnp.sum(fsum[q], axis=0, keepdims=True), 0.0)
 
 
 def greet(bricks):
@@ -133,17 +134,74 @@
     zs = (first,) if first == second else (first, second)
     return [(dx, dz) for dz in zs for dx in range(NX) if (dx, dz) != (0, 0)]
 
-def send_kernel(bricks, slots, seg, ship, feat, left, right, more, ext, stage, send_sem, recv_sems):
+def over_lanes(x, y):
+    return lax.dot_general(x.astype(BF16), y.astype(BF16), (((1,), (1,)), ((), ())), preferred_element_type=F32)
+
+def make_lists(kept, kept_count, lent, plan, lists):
+    region = lax.axis_index("region")
+    slots, regions, lend = kept.shape[1], plan.shape[0], lent.shape[2]
+    lane = lax.broadcasted_iota(jnp.int32, (1, slots), 1)
+    live = [lane < kept_count[0]]
+    ids = [[kept[0:1, :]], [kept[1:2, :]]]
+    step = lax.broadcasted_iota(jnp.int32, (1, lend), 1)
+    counts = plan[pl.ds(region, 1), :]
+    for j in range(regions):
+        live.append(step < jnp.broadcast_to(counts[:, j:j + 1], (1, lend)))
+        for side in range(2):
+            ids[side].append(lent[j, side:side + 1, :])
+    def ones(x):
+        return jnp.where(x, 1.0, 0.0)
+    live = jnp.concatenate([ones(x) for x in live], axis=1)
+    width = live.shape[1]
+    first, second = [jnp.concatenate([x.astype(F32) for x in ids[side]], axis=1) for side in range(2)]
+    row = lax.broadcasted_iota(jnp.int32, (width, width), 0)
+    col = lax.broadcasted_iota(jnp.int32, (width, width), 1)
+    wide = jnp.broadcast_to(live, (8, width))
+    before = over_lanes(wide, ones(col < row))[0:1]
+    total = over_lanes(wide, jnp.ones((width, width), F32))[0:1]
+    place = jnp.where(live > 0.0, before, -1.0)
+    pick = ones(jnp.broadcast_to(place, (width, width)).astype(jnp.int32) == row)
+    rows = jnp.concatenate([first, second, jnp.zeros((6, width), F32)], axis=0)
+    rows = over_lanes(rows, pick)
+    out = jnp.concatenate([rows[0:2], total, jnp.zeros((5, width), F32)], axis=0)
+    lists[...] = out.astype(jnp.int32)
+
+def make_owner(ship, owner):
+    leaves, ghosts = owner.shape
+    slots, bricks = ship.shape
+    leaf = lax.broadcasted_iota(jnp.int32, (leaves, bricks), 0)
+    here = [jnp.where(jnp.broadcast_to(ship[k:k + 1, :], (leaves, bricks)) == leaf, 1.0, 0.0) for k in range(slots)]
+    ghost = lax.broadcasted_iota(jnp.int32, (ghosts, bricks), 0)
+    brick = lax.broadcasted_iota(jnp.int32, (ghosts, bricks), 1)
+    total = 0.0
+    for k in range(slots):
+        total += over_lanes(here[k], jnp.where(ghost == brick * slots + k, 1.0, 0.0))
+    owner[...] = total.astype(BF16)
+
+def send_kernel(bricks, slots, seg_hbm, ship_hbm, kept_hbm, count, lent_hbm, plan_hbm,
+                feat, left, right, more, lists, owner, axes,
+                seg, ship, ship_rows, kept, lent, plan, ext, stage, in_sems, send_sem, recv_sems):
+    pairs = ((seg_hbm, seg), (ship_hbm, ship), (ship_hbm, ship_rows), (kept_hbm, kept),
+             (lent_hbm, lent), (plan_hbm, plan))
+    copies = [pltpu.make_async_copy(src, dst, in_sems.at[i]) for i, (src, dst) in enumerate(pairs)]
+    for copy in copies:
+        copy.start()
     me, barrier = greet(bricks)
     x, z = me // NZ, lax.rem(me, NZ)
     leaves = seg.shape[0]
+    for copy in copies[0:2]:
+        copy.wait()
     for q in range(bricks):
         for k in range(slots):
             stage[q * slots + k] = seg[ship[k, q]]
     origin = jnp.broadcast_to(seg[0, 0:3, 0:1], (3, 128))
     def own(i, _):
         for k in range(4):
-            prepare(seg[4 * i + k], origin, feat, left, right, more, 4 * i + k)
+            j = 4 * i + k
+            u, length = prepare(seg[j], origin, feat, left, right, more, j)
+            for q in range(3):
+                axes[q, pl.ds(j, 1), :] = u[q:q + 1]
+            axes[3, pl.ds(j, 1), :] = length
         return 0
     lax.fori_loop(0, leaves // 8, own, 0)
     pl.semaphore_wait(barrier, bricks - 1)
@@ -159,9 +217,13 @@
         for k in range(slots):
             prepare(source[q * slots + k], origin, feat, left, right, more, leaves + q * slots + k)
     ghosts(me, stage)
+    for copy in copies[2:]:
+        copy.wait()
+    make_lists(kept, count, lent, plan, lists)
+    make_owner(ship_rows, owner)
     for wave in range(len(WAVES)):
-        count = len(wave_offsets(wave)) * slots
-        pltpu.make_async_copy(stage.at[0:count], ext.at[0:count], recv_sems.at[wave]).wait()
+        count_in = len(wave_offsets(wave)) * slots
+        pltpu.make_async_copy(stage.at[0:count_in], ext.at[0:count_in], recv_sems.at[wave]).wait()
         first, second = WAVES[wave]
         skip = 1 if first == 0 else 0
         def arrived(i, _):
@@ -169,54 +231,40 @@
             q = lax.rem(x + NX - lax.rem(i, NX), NX) * NZ + lax.rem(z + NZ - dz, NZ)
             ghosts(q, ext)
             return 0
-        lax.fori_loop(skip, count // slots + skip, arrived, 0)
+        lax.fori_loop(skip, count_in // slots + skip, arrived, 0)
     total = (bricks - 1) * slots
     pltpu.make_async_copy(stage.at[0:total], ext.at[0:total], send_sem).wait()
 
 def back_kernel(bricks, slots, leaves, acc, back, send_sem, recv_sem):
     me, barrier = greet(bricks)
-    rows = slice(0, 6)
     pl.semaphore_wait(barrier, bricks - 1)
-    mine = back.at[pl.ds(me * slots, slots), rows]
+    mine = back.at[:, pl.ds(me * slots, slots)]
     for wave in range(len(WAVES)):
         for dx, dz in wave_offsets(wave):
             q = lax.rem(me // NZ + dx, NX) * NZ + lax.rem(me + dz, NZ)
             pltpu.make_async_remote_copy(
-                src_ref=acc.at[pl.ds(leaves + q * slots, slots), rows], dst_ref=mine, send_sem=send_sem, recv_sem=recv_sem,
+                src_ref=acc.at[:, pl.ds(leaves + q * slots, slots)], dst_ref=mine, send_sem=send_sem, recv_sem=recv_sem,
                 device_id={"brick": q}, device_id_type=MESH).start()
-    back[pl.ds(me * slots, slots)] = acc[pl.ds(leaves + me * slots, slots)]
+    for q in range(6):
+        back[q, pl.ds(me * slots, slots)] = acc[q, pl.ds(leaves + me * slots, slots)]
     total = (bricks - 1) * slots
-    pltpu.make_async_copy(acc.at[0:total, rows], back.at[0:total, rows], recv_sem).wait()
-    pltpu.make_async_copy(acc.at[0:total, rows], back.at[0:total, rows], send_sem).wait()
-
-def tile_kernel(kept, kept_count, lent, plan, feat, left, right, more, acc, ids_a, ids_b,
-                spread0, spread1, dots0, dots1, wide0, wide1, pend):
-    region = lax.axis_index("region")
-    spread0[...] = spread_matrix()
-    spread1[...] = spread_matrix()
-    acc[...] = jnp.zeros_like(acc)
-    pend[...] = jnp.zeros_like(pend)
-    n_kept = kept_count[0]
-    def list_kept(i, _):
-        ids_a[i] = kept[0, i]
-        ids_b[i] = kept[1, i]
-        return 0
-    lax.fori_loop(0, n_kept, list_kept, 0)
-    n = n_kept
-    for j in range(plan.shape[1]):
-        live = plan[region, j]
-        def list_lent(i, first, j=j):
-            ids_a[first + i] = lent[j, 0, i]
-            ids_b[first + i] = lent[j, 1, i]
-            return first
-        lax.fori_loop(0, live, list_lent, n)
-        n = n + live
+    pltpu.make_async_copy(acc.at[:, 0:total], back.at[:, 0:total], recv_sem).wait()
+    pltpu.make_async_copy(acc.at[:, 0:total], back.at[:, 0:total], send_sem).wait()
+
+UNROLL = 4
+
+def tile_kernel(lists, feat, left, right, more, acc, spread0, spread1, dots0, dots1, wide0, wide1, pend):
+    n = lists[2, 0]
     last = n - 1
     def at(t):
         t = jnp.minimum(t, last)
-        return ids_a[t], ids_b[t]
+        return lists[0, t], lists[1, t]
+    spread0[...] = spread_matrix()
+    spread1[...] = spread0[...]
     bufs = ((spread0, dots0, wide0), (spread1, dots1, wide1))
     products(*at(0), left, right, more, *bufs[0])
+    acc[...] = jnp.zeros_like(acc)
+    pend[...] = jnp.zeros_like(pend)
     lanes = lax.broadcasted_iota(jnp.int32, (8, 128), 1)
     diag = jnp.where(lanes % 8 == lax.broadcasted_iota(jnp.int32, (8, 128), 0), lanes // 8, -1)
     def tiles(first, count):
@@ -246,36 +294,26 @@
     lax.fori_loop(whole * (UNROLL // 2), pairs, few, 0)
     settle([pend[q] for q in range(18)], diag, acc, *at(2 * pairs - 1), True)
 
-UNROLL = 4
-
-def finish_kernel(slots, seg, ship, own, back, out, acc0, acc1, acc2, acc3):
-    accs = (acc0, acc1, acc2, acc3)
-    leaves = seg.shape[0]
-    acc0[...] = own[0:leaves]
-    for acc in accs[1:]:
-        acc[...] = jnp.zeros_like(acc)
-    bricks = back.shape[0] // slots
-    for q in range(bricks):
-        for k in range(slots):
-            acc = accs[k % 4]
-            leaf = ship[k, q]
-            acc[leaf, 0:6] += back[q * slots + k, 0:6]
-    for i in range(leaves):
-        total = acc0[i] + acc1[i] + acc2[i] + acc3[i]
-        d = [seg[i, 3 + q:4 + q] for q in range(3)]
-        a = d[0] * d[0] + d[1] * d[1] + d[2] * d[2]
-        inv = lax.rsqrt(a)
-        half = 0.5 * (a * inv)
-        u = [c * inv for c in d]
-        force = [total[q:q + 1] for q in range(3)]
-        lever = [total[3 + q:4 + q] - half * force[q] for q in range(3)]
-        torque = [u[(q + 1) % 3] * lever[(q + 2) % 3] - u[(q + 2) % 3] * lever[(q + 1) % 3] for q in range(3)]
-        for q in range(3):
-            out[q, i:i + 1] = force[q]
-            out[3 + q, i:i + 1] = torque[q]
+def finish_kernel(axes, owner, own, back, out):
+    leaves = out.shape[1]
+    pick = owner[...]
+    pick = jnp.concatenate([pick, pick, pick], axis=1)
+    total = []
+    for q in range(6):
+        parts = jnp.concatenate(split3(back[q]), axis=0).astype(BF16)
+        total.append(own[q, 0:leaves] + jnp.dot(pick, parts, preferred_element_type=F32))
+    u = [axes[q] for q in range(3)]
+    half = 0.5 * axes[3]
+    force = total[0:3]
+    lever = [total[3 + q] - half * force[q] for q in range(3)]
+    for q in range(3):
+        out[q] = force[q]
+        out[3 + q] = u[(q + 1) % 3] * lever[(q + 2) % 3] - u[(q + 2) % 3] * lever[(q + 1) % 3]
 
 VM = pl.BlockSpec(memory_space=pltpu.VMEM)
 SM = pl.BlockSpec(memory_space=pltpu.SMEM)
+HB = pl.BlockSpec(memory_space=pltpu.HBM)
+LIMIT = 26 * 2**20
 
 def body(segments, ship_list, kept_tiles, kept_count, lent_tiles, lent_count):
     leaves, _, width = segments.shape
@@ -285,49 +323,52 @@
     blocks = leaves + ghosts
     def shape(*s, dtype=F32):
         return jax.ShapeDtypeStruct(s, dtype)
+    def far(x):
+        return pltpu.with_memory_space_constraint(x, pltpu.HBM)
+    def room(x):
+        return pltpu.VMEM(x.shape, x.dtype)
     ship = jnp.transpose(ship_list[0], (1, 0))
     kept = jnp.transpose(kept_tiles[0], (1, 0))
     lent = jnp.transpose(lent_tiles[0], (0, 2, 1))
-    prepared = pl.pallas_call(
+    tile_slots = kept_tiles.shape[1] + lent_tiles.shape[1] * lent_tiles.shape[2]
+    feat, left, right, more, lists, owner, axes = pl.pallas_call(
         functools.partial(send_kernel, bricks, slots),
         out_shape=(shape(blocks, 8, width), shape(blocks, 128, 128, dtype=BF16), shape(blocks, 48, 384, dtype=BF16),
-                   shape(blocks, 16, 768, dtype=BF16)),
-        in_specs=[VM, SM], out_specs=(VM,) * 4,
-        scratch_shapes=[pltpu.VMEM((ghosts, 8, width), F32), pltpu.VMEM((ghosts, 8, width), F32),
-                        pltpu.SemaphoreType.DMA, pltpu.SemaphoreType.DMA((len(WAVES),))],
+                   shape(blocks, 16, 768, dtype=BF16), shape(8, tile_slots, dtype=jnp.int32),
+                   shape(leaves, ghosts, dtype=BF16), shape(4, leaves, width)),
+        in_specs=[HB] * 3 + [SM] + [HB] * 2, out_specs=(VM,) * 7,
+        scratch_shapes=[room(segments), pltpu.SMEM(ship.shape, jnp.int32), room(ship), room(kept), room(lent),
+                        pltpu.VMEM(lent_count.shape[1:], jnp.int32),
+                        pltpu.VMEM((ghosts, 8, width), F32), pltpu.VMEM((ghosts, 8, width), F32),
+                        pltpu.SemaphoreType.DMA((6,)), pltpu.SemaphoreType.DMA, pltpu.SemaphoreType.DMA((len(WAVES),))],
         compiler_params=pltpu.CompilerParams(collective_id=0, has_side_effects=True, vmem_limit_bytes=LIMIT),
-    )(segments, ship)
-    slots_total = kept_tiles.shape[1] + lent_tiles.shape[1] * lent_tiles.shape[2]
+    )(far(segments), far(ship), far(kept), kept_count, far(lent), far(lent_count[0]))
     acc = pl.pallas_call(
         tile_kernel,
-        out_shape=shape(blocks, 8, width),
-        in_specs=[SM] * 4 + [VM] * 4, out_specs=VM,
+        out_shape=shape(6, blocks, width),
+        in_specs=[SM] + [VM] * 4, out_specs=VM,
         scratch_shapes=[
-            pltpu.SMEM((slots_total,), jnp.int32), pltpu.SMEM((slots_total,), jnp.int32),
             pltpu.VMEM((128, 1280), BF16), pltpu.VMEM((128, 1280), BF16),
             pltpu.VMEM((128, 384), F32), pltpu.VMEM((128, 384), F32),
             pltpu.VMEM((128, 1280), F32), pltpu.VMEM((128, 1280), F32),
             pltpu.VMEM((18, 8, 128), F32),
         ],
         compiler_params=pltpu.CompilerParams(vmem_limit_bytes=LIMIT),
-    )(kept, kept_count, lent, lent_count[0], *prepared)
+    )(lists, feat, left, right, more)
     back = pl.pallas_call(
         functools.partial(back_kernel, bricks, slots, leaves),
-        out_shape=shape(ghosts, 8, width),
+        out_shape=shape(6, ghosts, width),
         in_specs=[VM], out_specs=VM,
         scratch_shapes=[pltpu.SemaphoreType.DMA, pltpu.SemaphoreType.DMA],
         compiler_params=pltpu.CompilerParams(collective_id=1, has_side_effects=True, vmem_limit_bytes=LIMIT),
     )(acc)
     loads = pl.pallas_call(
-        functools.partial(finish_kernel, slots),
+        finish_kernel,
         out_shape=shape(6, leaves, width),
-        in_specs=[VM, SM, VM, VM], out_specs=VM,
-        scratch_shapes=[pltpu.VMEM((leaves, 8, width), F32)] * 4,
+        in_specs=[VM] * 4, out_specs=VM,
         compiler_params=pltpu.CompilerParams(vmem_limit_bytes=LIMIT),
-    )(segments, ship, acc, back)
+    )(axes, owner, acc, back)
     return jnp.transpose(loads, (1, 0, 2))
-
-LIMIT = 26 * 2**20
 
 def solution(mesh):
     placed = (

time: 70 us -> 63.3 us (0.904); the launches traced: 69.8 us -> 62.3 us
  Pallas kernels: 65.4 us -> 61.6 us
  local copies, waits for them, and re-layouts: 3.64 us -> 0 us
    pallas_call x2, Pallas kernels: 23.1 us -> 12.1 us  [the longest x1 11.2 us: body(): pl.pallas_call(tile_kernel, out_shape=shape(6, blocks, width), in_specs=[...]
    pallas_call x1, Pallas kernels: 18 us -> 25.6 us  [body(): pl.pallas_call(functools.partial(back_kernel, bricks, slots, leaves), out...]
    unnamed x10 -> x0, local copies, waits for them, and re-layouts: 3.64 us -> none
where the time goes in v3:
time: 63.3 us; the launch traced here: 62.3 us
  Pallas kernels  61.6 us (97%)
  between operations  0.67 us (1%)
    pallas_call x1, Pallas kernels, body(): pl.pallas_call(functools.partial(back_kernel, bricks, slots, leaves), out...  25.6 us
    pallas_call x1, Pallas kernels, body(): pl.pallas_call(functools.partial(send_kernel, bricks, slots), out_shape=(...  24 us
    pallas_call x1, Pallas kernels, body(): pl.pallas_call(tile_kernel, out_shape=shape(6, blocks, width), in_specs=[...  11.2 us

profile of v3, /device:TPU:24, one launch (start us, length us, event | category | flops | bytes accessed | tf_op | source)
XLA Modules:
  0.0 62.3 jit_solution(5152686081382823880)
XLA Ops:
  0.7 24.0 %shard_map.64 = (f32[160,8,128]{2,1,0:T(8,128)S(1)}, bf16[160,128,128]{2,1,0:T(8,128)(2,1)S(1)}, bf16[160,48,384]{2,1,0:T(8,128)(2,1)S(1)}, bf16[160,16,768]{2,1...) custom-call(f32[32,8,128]{2,1,0:T(8,128)} %seg_hbm.1, ...), custom_call_target="tpu_custom_call" | custom-call | tf_op jit(solution)/shard_map/pallas_call | solution.py:334
  24.6 11.2 %shard_map.65.acc.own = f32[6,160,128]{2,1,0:T(8,128)S(1)} custom-call(s32[8,128]{1,0:T(8,128)S(1)} %get-tuple-element.14.lists, f32[160,8,128]{2,1,0:T(8,128)S(1)} %get-tuple-element.15.feat, bf16[160,128,128]{2,1,0:T(8,128)(2,1)S(1)} %get-tuple-element.16.left, bf16[160,48,384]{2,1,0:T(8,128)(2,1)S(1)} %get-tuple-element.17.right, ...), custom_call_target="tpu_custom_call" | custom-call | tf_op jit(solution)/shard_map/pallas_call | solution.py:346
  35.8 25.6 %shard_map.66.back = f32[6,128,128]{2,1,0:T(8,128)S(1)} custom-call(f32[6,160,128]{2,1,0:T(8,128)S(1)} %shard_map.65.acc.own), custom_call_target="tpu_custom_call" | custom-call | tf_op jit(solution)/shard_map/pallas_call | solution.py:358
  61.4 0.9 %shard_map.67 = f32[6,32,128]{2,1,0:T(8,128)} custom-call(f32[4,32,128]{2,1,0:T(8,128)S(1)} %get-tuple-element.12.axes, bf16[32,128]{1,0:T(8,128)(2,1)S(1)} %get-tuple-element.13.owner, f32[6,160,128]{2,1,0:T(8,128)S(1)} %shard_map.65.acc.own, f32[6,128,128]{2,1,0:T(8,128)S(1)} %shard_map.66.back), custom_call_target="tpu_custom_call" | custom-call | tf_op jit(solution)/shard_map/pallas_call | solution.py:365

commit v4 on v3

--- a/solution.py
+++ b/solution.py
@@ -108,16 +108,21 @@
             fsum[q] = back[q] if g == 0 else fsum[q] + back[q]
     return vals + asum + fsum
 
+def diagonal():
+    lanes = lax.broadcasted_iota(jnp.int32, (8, 128), 1)
+    return jnp.where(lanes % 8 == lax.broadcasted_iota(jnp.int32, (8, 128), 0), lanes // 8, -1)
+
+def reduced(pending, diag):
+    vals, asum, fsum = pending[0:6], pending[6:12], pending[12:18]
+    last = [jnp.where(diag == 15, jnp.sum(vals[q], axis=1, keepdims=True), asum[q]) for q in range(6)]
+    return [jnp.sum(x, axis=0, keepdims=True) for x in last], [jnp.sum(x, axis=0, keepdims=True) for x in fsum]
+
 def settle(pending, diag, acc, a, b, live):
-    vals, asum, fsum = pending[0:6], pending[6:12], pending[12:18]
-    for q in range(6):
-        red = jnp.sum(vals[q], axis=1, keepdims=True)
-        asum[q] = jnp.where(diag == 15, red, asum[q])
-    for q in range(6):
-        acc[q, pl.ds(a, 1), :] += jnp.where(live, jnp.sum(asum[q], axis=0, keepdims=True), 0.0)
-    for q in range(6):
-        acc[q, pl.ds(b, 1), :] -= jnp.where(live, jnp.sum(fsum[q], axis=0, keepdims=True), 0.0)
-
+    asum, fsum = reduced(pending, diag)
+    for q in range(6):
+        acc[q, pl.ds(a, 1), :] += jnp.where(live, asum[q], 0.0)
+    for q in range(6):
+        acc[q, pl.ds(b, 1), :] -= jnp.where(live, fsum[q], 0.0)
 
 def greet(bricks):
     me = lax.axis_index("brick")
@@ -137,7 +142,9 @@
 def over_lanes(x, y):
     return lax.dot_general(x.astype(BF16), y.astype(BF16), (((1,), (1,)), ((), ())), preferred_element_type=F32)
 
-def make_lists(kept, kept_count, lent, plan, lists):
+LATE = 24
+
+def make_lists(leaves, slots_out, kept, kept_count, lent, plan, lists):
     region = lax.axis_index("region")
     slots, regions, lend = kept.shape[1], plan.shape[0], lent.shape[2]
     lane = lax.broadcasted_iota(jnp.int32, (1, slots), 1)
@@ -156,14 +163,22 @@
     first, second = [jnp.concatenate([x.astype(F32) for x in ids[side]], axis=1) for side in range(2)]
     row = lax.broadcasted_iota(jnp.int32, (width, width), 0)
     col = lax.broadcasted_iota(jnp.int32, (width, width), 1)
-    wide = jnp.broadcast_to(live, (8, width))
-    before = over_lanes(wide, ones(col < row))[0:1]
-    total = over_lanes(wide, jnp.ones((width, width), F32))[0:1]
-    place = jnp.where(live > 0.0, before, -1.0)
-    pick = ones(jnp.broadcast_to(place, (width, width)).astype(jnp.int32) == row)
-    rows = jnp.concatenate([first, second, jnp.zeros((6, width), F32)], axis=0)
-    rows = over_lanes(rows, pick)
-    out = jnp.concatenate([rows[0:2], total, jnp.zeros((5, width), F32)], axis=0)
+    def inner(v):
+        return jnp.where((v >= leaves) & (lax.rem(v, slots_out) >= slots_out // 2), 0.0, 1.0)
+    inside = live * inner(first.astype(jnp.int32)) * inner(second.astype(jnp.int32))
+    def before(flags):
+        return over_lanes(jnp.broadcast_to(flags, (8, width)), ones(col < row))[0:1]
+    late = jnp.where(before(inside) < LATE, inside, 0.0)
+    now = live - late
+    total = over_lanes(jnp.broadcast_to(now, (8, width)), jnp.ones((width, width), F32))[0:1]
+    def moved(values, flags, shift):
+        place = jnp.where(flags > 0.0, before(flags) + shift, -1.0).astype(jnp.int32)
+        pick = ones(jnp.broadcast_to(place, (width, width)) == row)
+        return over_lanes(jnp.broadcast_to(values, (8, width)), pick)[0:1]
+    late_a, late_b = moved(first + 1.0, late, 1), moved(second + 1.0, late, 1)
+    places = late_a + moved(second + 1.0, late, 1 + width // 2) - 1.0
+    out = jnp.concatenate([moved(first, now, 0), moved(second, now, 0), total, jnp.maximum(late_a - 1.0, 0.0),
+                           jnp.maximum(late_b - 1.0, 0.0), places, jnp.zeros((2, width), F32)], axis=0)
     lists[...] = out.astype(jnp.int32)
 
 def make_owner(ship, owner):
@@ -219,7 +234,7 @@
     ghosts(me, stage)
     for copy in copies[2:]:
         copy.wait()
-    make_lists(kept, count, lent, plan, lists)
+    make_lists(leaves, slots, kept, count, lent, plan, lists)
     make_owner(ship_rows, owner)
     for wave in range(len(WAVES)):
         count_in = len(wave_offsets(wave)) * slots
@@ -235,29 +250,76 @@
     total = (bricks - 1) * slots
     pltpu.make_async_copy(stage.at[0:total], ext.at[0:total], send_sem).wait()
 
-def back_kernel(bricks, slots, leaves, acc, back, send_sem, recv_sem):
+def back_kernel(bricks, slots, leaves, lists, places, feat, left, right, more, acc, own, back, total, sums,
+                spread0, spread1, dots0, dots1, wide0, wide1, pend, send_sem, recv_sems):
     me, barrier = greet(bricks)
+    def at(t):
+        t = jnp.minimum(t + 1, LATE)
+        return lists[3, t], lists[4, t]
+    spread0[...] = spread_matrix()
+    spread1[...] = spread0[...]
+    bufs = ((spread0, dots0, wide0), (spread1, dots1, wide1))
+    products(*at(0), left, right, more, *bufs[0])
+    pend[...] = jnp.zeros_like(pend)
+    sums[...] = jnp.zeros_like(sums)
+    diag = diagonal()
+    def keep(pending, row):
+        asum, fsum = reduced(pending, diag)
+        for q in range(6):
+            sums[q, pl.ds(row, 1), :] = asum[q]
+            sums[q, pl.ds(row + 64, 1), :] = -fsum[q]
+    def some(i, _):
+        for k in range(LATE_UNROLL):
+            t = LATE_UNROLL * i + k
+            _, b = at(t)
+            products(*at(t + 1), left, right, more, *bufs[(k + 1) % 2])
+            if k == 0:
+                pending = [pend[q] for q in range(18)]
+            keep(pending, t)
+            pending = tile(b, feat, *bufs[k % 2][1:], diag)
+        for q in range(18):
+            pend[q] = pending[q]
+        return 0
+    half = slots // 2
+    def send(half_number, source):
+        mine = back.at[:, pl.ds(me * slots + half_number * half, half)]
+        for wave in range(len(WAVES)):
+            for dx, dz in wave_offsets(wave):
+                q = lax.rem(me // NZ + dx, NX) * NZ + lax.rem(me + dz, NZ)
+                pltpu.make_async_remote_copy(
+                    src_ref=source.at[:, pl.ds(leaves + q * slots + half_number * half, half)], dst_ref=mine,
+                    send_sem=send_sem, recv_sem=recv_sems.at[half_number], device_id={"brick": q}, device_id_type=MESH).start()
+    lax.fori_loop(0, EARLY // LATE_UNROLL, some, 0)
     pl.semaphore_wait(barrier, bricks - 1)
-    mine = back.at[:, pl.ds(me * slots, slots)]
-    for wave in range(len(WAVES)):
-        for dx, dz in wave_offsets(wave):
-            q = lax.rem(me // NZ + dx, NX) * NZ + lax.rem(me + dz, NZ)
-            pltpu.make_async_remote_copy(
-                src_ref=acc.at[:, pl.ds(leaves + q * slots, slots)], dst_ref=mine, send_sem=send_sem, recv_sem=recv_sem,
-                device_id={"brick": q}, device_id_type=MESH).start()
-    for q in range(6):
-        back[q, pl.ds(me * slots, slots)] = acc[q, pl.ds(leaves + me * slots, slots)]
-    total = (bricks - 1) * slots
-    pltpu.make_async_copy(acc.at[:, 0:total], back.at[:, 0:total], recv_sem).wait()
-    pltpu.make_async_copy(acc.at[:, 0:total], back.at[:, 0:total], send_sem).wait()
-
+    send(1, acc)
+    lax.fori_loop(EARLY // LATE_UNROLL, LATE // LATE_UNROLL, some, 0)
+    keep([pend[q] for q in range(18)], LATE)
+    blocks = total.shape[1]
+    pick = jnp.where(lax.broadcasted_iota(jnp.int32, (blocks, 128), 0) == jnp.broadcast_to(places[5:6, :], (blocks, 128)), 1.0, 0.0)
+    pick = pick.astype(BF16)
+    pick = jnp.concatenate([pick, pick, pick], axis=1)
+    for q in range(6):
+        parts = jnp.concatenate(split3(sums[q]), axis=0).astype(BF16)
+        total[q] = acc[q] + jnp.dot(pick, parts, preferred_element_type=F32)
+    send(0, total)
+    own[...] = total[:, 0:leaves]
+    for q in range(6):
+        back[q, pl.ds(me * slots, half)] = total[q, pl.ds(leaves + me * slots, half)]
+        back[q, pl.ds(me * slots + half, half)] = acc[q, pl.ds(leaves + me * slots + half, half)]
+    sent = (bricks - 1) * half
+    for half_number in range(2):
+        pltpu.make_async_copy(acc.at[:, 0:sent], back.at[:, 0:sent], recv_sems.at[half_number]).wait()
+    pltpu.make_async_copy(acc.at[:, 0:2 * sent], back.at[:, 0:2 * sent], send_sem).wait()
+
+LATE_UNROLL = 4
+EARLY = 8
 UNROLL = 4
 
 def tile_kernel(lists, feat, left, right, more, acc, spread0, spread1, dots0, dots1, wide0, wide1, pend):
     n = lists[2, 0]
-    last = n - 1
+    last = jnp.maximum(n - 1, 0)
     def at(t):
-        t = jnp.minimum(t, last)
+        t = jnp.minimum(jnp.maximum(t, 0), last)
         return lists[0, t], lists[1, t]
     spread0[...] = spread_matrix()
     spread1[...] = spread0[...]
@@ -265,8 +327,7 @@
     products(*at(0), left, right, more, *bufs[0])
     acc[...] = jnp.zeros_like(acc)
     pend[...] = jnp.zeros_like(pend)
-    lanes = lax.broadcasted_iota(jnp.int32, (8, 128), 1)
-    diag = jnp.where(lanes % 8 == lax.broadcasted_iota(jnp.int32, (8, 128), 0), lanes // 8, -1)
+    diag = diagonal()
     def tiles(first, count):
         for k in range(count):
             t = first + k
@@ -274,7 +335,7 @@
             products(*at(t + 1), left, right, more, *bufs[(k + 1) % 2])
             if k == 0:
                 pending = [pend[q] for q in range(18)]
-                before = at(jnp.maximum(t - 1, 0))
+                before = at(t - 1)
                 live = True
             settle(pending, diag, acc, *before, live)
             pending = tile(b, feat, *bufs[k % 2][1:], diag)
@@ -301,7 +362,7 @@
     total = []
     for q in range(6):
         parts = jnp.concatenate(split3(back[q]), axis=0).astype(BF16)
-        total.append(own[q, 0:leaves] + jnp.dot(pick, parts, preferred_element_type=F32))
+        total.append(own[q] + jnp.dot(pick, parts, preferred_element_type=F32))
     u = [axes[q] for q in range(3)]
     half = 0.5 * axes[3]
     force = total[0:3]
@@ -343,31 +404,33 @@
                         pltpu.SemaphoreType.DMA((6,)), pltpu.SemaphoreType.DMA, pltpu.SemaphoreType.DMA((len(WAVES),))],
         compiler_params=pltpu.CompilerParams(collective_id=0, has_side_effects=True, vmem_limit_bytes=LIMIT),
     )(far(segments), far(ship), far(kept), kept_count, far(lent), far(lent_count[0]))
+    buffers = [
+        pltpu.VMEM((128, 1280), BF16), pltpu.VMEM((128, 1280), BF16),
+        pltpu.VMEM((128, 384), F32), pltpu.VMEM((128, 384), F32),
+        pltpu.VMEM((128, 1280), F32), pltpu.VMEM((128, 1280), F32),
+        pltpu.VMEM((18, 8, 128), F32),
+    ]
     acc = pl.pallas_call(
         tile_kernel,
         out_shape=shape(6, blocks, width),
         in_specs=[SM] + [VM] * 4, out_specs=VM,
-        scratch_shapes=[
-            pltpu.VMEM((128, 1280), BF16), pltpu.VMEM((128, 1280), BF16),
-            pltpu.VMEM((128, 384), F32), pltpu.VMEM((128, 384), F32),
-            pltpu.VMEM((128, 1280), F32), pltpu.VMEM((128, 1280), F32),
-            pltpu.VMEM((18, 8, 128), F32),
-        ],
+        scratch_shapes=buffers,
         compiler_params=pltpu.CompilerParams(vmem_limit_bytes=LIMIT),
     )(lists, feat, left, right, more)
-    back = pl.pallas_call(
+    own, back = pl.pallas_call(
         functools.partial(back_kernel, bricks, slots, leaves),
-        out_shape=shape(6, ghosts, width),
-        in_specs=[VM], out_specs=VM,
-        scratch_shapes=[pltpu.SemaphoreType.DMA, pltpu.SemaphoreType.DMA],
+        out_shape=(shape(6, leaves, width), shape(6, ghosts, width)),
+        in_specs=[SM] + [VM] * 6, out_specs=(VM, VM),
+        scratch_shapes=[pltpu.VMEM((6, blocks, width), F32), pltpu.VMEM((6, 128, width), F32)] + buffers
+        + [pltpu.SemaphoreType.DMA, pltpu.SemaphoreType.DMA((2,))],
         compiler_params=pltpu.CompilerParams(collective_id=1, has_side_effects=True, vmem_limit_bytes=LIMIT),
-    )(acc)
+    )(lists, lists, feat, left, right, more, acc)
     loads = pl.pallas_call(
         finish_kernel,
         out_shape=shape(6, leaves, width),
         in_specs=[VM] * 4, out_specs=VM,
         compiler_params=pltpu.CompilerParams(vmem_limit_bytes=LIMIT),
-    )(axes, owner, acc, back)
+    )(axes, owner, own, back)
     return jnp.transpose(loads, (1, 0, 2))
 
 def solution(mesh):

time: 63.3 us -> 60.8 us (0.961)
  the two profiles are of different devices: /device:TPU:24 before, /device:TPU:32 now
where the time goes in v4:
time: 60.8 us; the launch traced here: 60.7 us
  Pallas kernels  60 us (99%)
  between operations  0.67 us (1%)
    pallas_call x1, Pallas kernels, body(): pl.pallas_call(functools.partial(back_kernel, bricks, slots, leaves), out...  27.2 us
    pallas_call x1, Pallas kernels, body(): pl.pallas_call(functools.partial(send_kernel, bricks, slots), out_shape=(...  23.6 us
    pallas_call x1, Pallas kernels, body(): pl.pallas_call(tile_kernel, out_shape=shape(6, blocks, width), in_specs=[...  8.26 us

profile of v4, /device:TPU:32, one launch (start us, length us, event | category | flops | bytes accessed | tf_op | source)
XLA Modules:
  0.0 60.7 jit_solution(11635932638703506550)
XLA Ops:
  0.7 23.6 %shard_map.64 = (f32[160,8,128]{2,1,0:T(8,128)S(1)}, bf16[160,128,128]{2,1,0:T(8,128)(2,1)S(1)}, bf16[160,48,384]{2,1,0:T(8,128)(2,1)S(1)}, bf16[160,16,768]{2,1...) custom-call(f32[32,8,128]{2,1,0:T(8,128)} %seg_hbm.1, ...), custom_call_target="tpu_custom_call" | custom-call | tf_op jit(solution)/shard_map/pallas_call | solution.py:395
  24.3 8.3 %shard_map.65.acc = f32[6,160,128]{2,1,0:T(8,128)S(1)} custom-call(s32[8,128]{1,0:T(8,128)S(1)} %get-tuple-element.16.lists.places, f32[160,8,128]{2,1,0:T(8,128)S(1)} %get-tuple-element.17.feat, bf16[160,128,128]{2,1,0:T(8,128)(2,1)S(1)} %get-tuple-element.18.left, bf16[160,48,384]{2,1,0:T(8,128)(2,1)S(1)} %get-tuple-element.19.right, ...), custom_call_target="tpu_custom_call" | custom-call | tf_op jit(solution)/shard_map/pallas_call | solution.py:413
  32.5 27.2 %shard_map.66 = (f32[6,32,128]{2,1,0:T(8,128)S(1)}, f32[6,128,128]{2,1,0:T(8,128)S(1)}) custom-call(s32[8,128]{1,0:T(8,128)S(1)} %get-tuple-element.16.lists.places, s32[8,128]{1,0:T(8,128)S(1)} %get-tuple-element.16.lists.places, f32[160,8,128]{2,1,0:T(8,128)S(1)} %get-tuple-element.17.feat, bf16[160,128,128]{2,1,0:T(8,128)(2,1)S(1)} %get-tuple-element.18.left, ...), custom_call_target="tpu_custom_call" | custom-call | tf_op jit(solution)/shard_map/pallas_call | solution.py:420
  59.8 0.9 %shard_map.67 = f32[6,32,128]{2,1,0:T(8,128)} custom-call(f32[4,32,128]{2,1,0:T(8,128)S(1)} %get-tuple-element.14.axes, bf16[32,128]{1,0:T(8,128)(2,1)S(1)} %get-tuple-element.15.owner, f32[6,32,128]{2,1,0:T(8,128)S(1)} %get-tuple-element.21.own, f32[6,128,128]{2,1,0:T(8,128)S(1)} %get-tuple-element.22.back), custom_call_target="tpu_custom_call" | custom-call | tf_op jit(solution)/shard_map/pallas_call | solution.py:428

commit v5 on v4

--- a/solution.py
+++ b/solution.py
@@ -283,7 +283,7 @@
     half = slots // 2
     def send(half_number, source):
         mine = back.at[:, pl.ds(me * slots + half_number * half, half)]
-        for wave in range(len(WAVES)):
+        for wave in reversed(range(len(WAVES))):
             for dx, dz in wave_offsets(wave):
                 q = lax.rem(me // NZ + dx, NX) * NZ + lax.rem(me + dz, NZ)
                 pltpu.make_async_remote_copy(
@@ -312,8 +312,8 @@
     pltpu.make_async_copy(acc.at[:, 0:2 * sent], back.at[:, 0:2 * sent], send_sem).wait()
 
 LATE_UNROLL = 4
-EARLY = 8
-UNROLL = 4
+EARLY = 12
+UNROLL = 6
 
 def tile_kernel(lists, feat, left, right, more, acc, spread0, spread1, dots0, dots1, wide0, wide1, pend):
     n = lists[2, 0]

time: 60.8 us -> 60 us (0.987)
  the two profiles are of different devices: /device:TPU:32 before, /device:TPU:24 now
where the time goes in v5:
time: 60 us; the launch traced here: 59.1 us
  Pallas kernels  58.4 us (97%)
  between operations  0.67 us (1%)
    pallas_call x1, Pallas kernels, body(): pl.pallas_call(functools.partial(back_kernel, bricks, slots, leaves), out...  27.9 us
    pallas_call x1, Pallas kernels, body(): pl.pallas_call(functools.partial(send_kernel, bricks, slots), out_shape=(...  24 us
    pallas_call x1, Pallas kernels, body(): pl.pallas_call(tile_kernel, out_shape=shape(6, blocks, width), in_specs=[...  5.68 us

profile of v5, /device:TPU:24, one launch (start us, length us, event | category | flops | bytes accessed | tf_op | source)
XLA Modules:
  0.0 59.1 jit_solution(6660854555431970894)
XLA Ops:
  0.7 24.0 %shard_map.64 = (f32[160,8,128]{2,1,0:T(8,128)S(1)}, bf16[160,128,128]{2,1,0:T(8,128)(2,1)S(1)}, bf16[160,48,384]{2,1,0:T(8,128)(2,1)S(1)}, bf16[160,16,768]{2,1...) custom-call(f32[32,8,128]{2,1,0:T(8,128)} %seg_hbm.1, ...), custom_call_target="tpu_custom_call" | custom-call | tf_op jit(solution)/shard_map/pallas_call | solution.py:395
  24.7 5.7 %shard_map.65.acc = f32[6,160,128]{2,1,0:T(8,128)S(1)} custom-call(s32[8,128]{1,0:T(8,128)S(1)} %get-tuple-element.16.lists.places, f32[160,8,128]{2,1,0:T(8,128)S(1)} %get-tuple-element.17.feat, bf16[160,128,128]{2,1,0:T(8,128)(2,1)S(1)} %get-tuple-element.18.left, bf16[160,48,384]{2,1,0:T(8,128)(2,1)S(1)} %get-tuple-element.19.right, ...), custom_call_target="tpu_custom_call" | custom-call | tf_op jit(solution)/shard_map/pallas_call | solution.py:413
  30.3 27.9 %shard_map.66 = (f32[6,32,128]{2,1,0:T(8,128)S(1)}, f32[6,128,128]{2,1,0:T(8,128)S(1)}) custom-call(s32[8,128]{1,0:T(8,128)S(1)} %get-tuple-element.16.lists.places, s32[8,128]{1,0:T(8,128)S(1)} %get-tuple-element.16.lists.places, f32[160,8,128]{2,1,0:T(8,128)S(1)} %get-tuple-element.17.feat, bf16[160,128,128]{2,1,0:T(8,128)(2,1)S(1)} %get-tuple-element.18.left, ...), custom_call_target="tpu_custom_call" | custom-call | tf_op jit(solution)/shard_map/pallas_call | solution.py:420
  58.2 0.9 %shard_map.67 = f32[6,32,128]{2,1,0:T(8,128)} custom-call(f32[4,32,128]{2,1,0:T(8,128)S(1)} %get-tuple-element.14.axes, bf16[32,128]{1,0:T(8,128)(2,1)S(1)} %get-tuple-element.15.owner, f32[6,32,128]{2,1,0:T(8,128)S(1)} %get-tuple-element.21.own, f32[6,128,128]{2,1,0:T(8,128)S(1)} %get-tuple-element.22.back), custom_call_target="tpu_custom_call" | custom-call | tf_op jit(solution)/shard_map/pallas_call | solution.py:428

commit v6 on v5

--- a/solution.py
+++ b/solution.py
@@ -36,7 +36,7 @@
     h1, m1, l1 = split3(x1)
     h2, m2, l2 = split3(x2)
     rows = jnp.concatenate([h1, h1, m1, m1, h1, l1, h2, m2, l2, jnp.ones((8, 128), F32), jnp.zeros((128 - 80, 128), F32)], axis=0)
-    left[blk] = rows.T.astype(BF16)
+    left[blk] = rows.astype(BF16).T
     for q, x in enumerate(extra(p, r, ir, ie)):
         more[blk, :, 128 * q:128 * q + 128] = x
     z = jnp.zeros((3, 128), F32)
@@ -211,14 +211,14 @@
             stage[q * slots + k] = seg[ship[k, q]]
     origin = jnp.broadcast_to(seg[0, 0:3, 0:1], (3, 128))
     def own(i, _):
-        for k in range(4):
-            j = 4 * i + k
+        for k in range(8):
+            j = 8 * i + k
             u, length = prepare(seg[j], origin, feat, left, right, more, j)
             for q in range(3):
                 axes[q, pl.ds(j, 1), :] = u[q:q + 1]
             axes[3, pl.ds(j, 1), :] = length
         return 0
-    lax.fori_loop(0, leaves // 8, own, 0)
+    lax.fori_loop(0, leaves // 16, own, 0)
     pl.semaphore_wait(barrier, bricks - 1)
     mine = ext.at[pl.ds(me * slots, slots)]
     for wave in range(len(WAVES)):
@@ -227,7 +227,7 @@
             pltpu.make_async_remote_copy(
                 src_ref=stage.at[pl.ds(q * slots, slots)], dst_ref=mine, send_sem=send_sem, recv_sem=recv_sems.at[wave],
                 device_id={"brick": q}, device_id_type=MESH).start()
-    lax.fori_loop(leaves // 8, leaves // 4, own, 0)
+    lax.fori_loop(leaves // 16, leaves // 8, own, 0)
     def ghosts(q, source):
         for k in range(slots):
             prepare(source[q * slots + k], origin, feat, left, right, more, leaves + q * slots + k)
@@ -240,13 +240,16 @@
         count_in = len(wave_offsets(wave)) * slots
         pltpu.make_async_copy(stage.at[0:count_in], ext.at[0:count_in], recv_sems.at[wave]).wait()
         first, second = WAVES[wave]
-        skip = 1 if first == 0 else 0
+        def source(i):
+            dz = first + (second - first) * (i // NX)
+            return lax.rem(x + NX - lax.rem(i, NX), NX) * NZ + lax.rem(z + NZ - dz, NZ)
         def arrived(i, _):
-            dz = first + (second - first) * (i // NX)
-            q = lax.rem(x + NX - lax.rem(i, NX), NX) * NZ + lax.rem(z + NZ - dz, NZ)
-            ghosts(q, ext)
+            ghosts(source(2 * i), ext)
+            ghosts(source(2 * i + 1), ext)
             return 0
-        lax.fori_loop(skip, count_in // slots + skip, arrived, 0)
+        if first == 0:
+            ghosts(source(1), ext)
+        lax.fori_loop(1 if first == 0 else 0, (count_in // slots + 1) // 2, arrived, 0)
     total = (bricks - 1) * slots
     pltpu.make_async_copy(stage.at[0:total], ext.at[0:total], send_sem).wait()
 

time: 60 us -> 58.7 us (0.978)
  Pallas kernels: 58.4 us -> 57.4 us
    pallas_call x1, Pallas kernels: 24 us -> 23.3 us  [body(): pl.pallas_call(functools.partial(send_kernel, bricks, slots), out_shape=(...]
where the time goes in v6:
time: 58.7 us; the launch traced here: 58.1 us
  Pallas kernels  57.4 us (98%)
  between operations  0.67 us (1%)
    pallas_call x1, Pallas kernels, body(): pl.pallas_call(functools.partial(back_kernel, bricks, slots, leaves), out...  27.5 us
    pallas_call x1, Pallas kernels, body(): pl.pallas_call(functools.partial(send_kernel, bricks, slots), out_shape=(...  23.3 us
    pallas_call x1, Pallas kernels, body(): pl.pallas_call(tile_kernel, out_shape=shape(6, blocks, width), in_specs=[...  5.67 us

profile of v6, /device:TPU:24, one launch (start us, length us, event | category | flops | bytes accessed | tf_op | source)
XLA Modules:
  0.0 58.1 jit_solution(7601891559209192864)
XLA Ops:
  0.7 23.3 %shard_map.64 = (f32[160,8,128]{2,1,0:T(8,128)S(1)}, bf16[160,128,128]{2,1,0:T(8,128)(2,1)S(1)}, bf16[160,48,384]{2,1,0:T(8,128)(2,1)S(1)}, bf16[160,16,768]{2,1...) custom-call(f32[32,8,128]{2,1,0:T(8,128)} %seg_hbm.1, ...), custom_call_target="tpu_custom_call" | custom-call | tf_op jit(solution)/shard_map/pallas_call | solution.py:398
  24.0 5.7 %shard_map.65.acc = f32[6,160,128]{2,1,0:T(8,128)S(1)} custom-call(s32[8,128]{1,0:T(8,128)S(1)} %get-tuple-element.16.lists.places, f32[160,8,128]{2,1,0:T(8,128)S(1)} %get-tuple-element.17.feat, bf16[160,128,128]{2,1,0:T(8,128)(2,1)S(1)} %get-tuple-element.18.left, bf16[160,48,384]{2,1,0:T(8,128)(2,1)S(1)} %get-tuple-element.19.right, ...), custom_call_target="tpu_custom_call" | custom-call | tf_op jit(solution)/shard_map/pallas_call | solution.py:416
  29.7 27.5 %shard_map.66 = (f32[6,32,128]{2,1,0:T(8,128)S(1)}, f32[6,128,128]{2,1,0:T(8,128)S(1)}) custom-call(s32[8,128]{1,0:T(8,128)S(1)} %get-tuple-element.16.lists.places, s32[8,128]{1,0:T(8,128)S(1)} %get-tuple-element.16.lists.places, f32[160,8,128]{2,1,0:T(8,128)S(1)} %get-tuple-element.17.feat, bf16[160,128,128]{2,1,0:T(8,128)(2,1)S(1)} %get-tuple-element.18.left, ...), custom_call_target="tpu_custom_call" | custom-call | tf_op jit(solution)/shard_map/pallas_call | solution.py:423
  57.2 0.9 %shard_map.67 = f32[6,32,128]{2,1,0:T(8,128)} custom-call(f32[4,32,128]{2,1,0:T(8,128)S(1)} %get-tuple-element.14.axes, bf16[32,128]{1,0:T(8,128)(2,1)S(1)} %get-tuple-element.15.owner, f32[6,32,128]{2,1,0:T(8,128)S(1)} %get-tuple-element.21.own, f32[6,128,128]{2,1,0:T(8,128)S(1)} %get-tuple-element.22.back), custom_call_target="tpu_custom_call" | custom-call | tf_op jit(solution)/shard_map/pallas_call | solution.py:431
